TPU v7x, 32 devices: a whole 2x2x4 slice. The times are simulated.
32 devices in a mesh: ctx: 8 (over z, x), chan: 4 (over y, core).
Axes of the slice: x: 2, y: 2, z: 4, core: 2. Of those that a mesh axis runs over, the one named last changes fastest.
Arguments:
- signal: bfloat16 [128, 8192], P('chan', 'ctx'), may hold values from -6 to 6
- gating: bfloat16 [128, 8192], P('chan', 'ctx'), may hold values from -6 to 6
- cotangent: bfloat16 [128, 8192], P('chan', 'ctx'), may hold values from -6 to 6
- filters: float32 [32, 8192], P(None, 'ctx'), may hold values from -1 to 1
- skip_weight: float32 [128], P('chan'), may hold values from 0.5 to 1.5
Outputs:
- grad_signal: bfloat16 [128, 8192], P('chan', 'ctx')
- grad_gating: bfloat16 [128, 8192], P('chan', 'ctx')
- grad_filters: float32 [32, 8192], P('chan', 'ctx')
All inputs are finite; a program needn't handle non-finite values.
Results may differ from a plain program's by a relative error of at most 0.0075.
Values may be sent and summed in bfloat16 or wider, within the bound.
No kernel may reach another device: no remote copies, remote signals or barrier semaphores. Data moves between devices by JAX's collectives and lax.ppermute only.
A program may use at most 64 MiB of HBM per device.

v0:
```python
import math

import jax
import jax.numpy as jnp
from jax import lax
from jax.sharding import PartitionSpec as P


def product(form, left, right):
    return jnp.einsum(
        form, left, right, precision=lax.Precision.HIGHEST, preferred_element_type=jnp.float32
    )


def phases(left_idx, right_idx, period):
    joined = left_idx[:, None] * right_idx[None, :] % period
    return joined.astype(jnp.float32) * (2.0 * math.pi / period)


def indices(total):
    return jnp.arange(total, dtype=jnp.int32)


def turn_forward(real_part, imag_part, angles):
    cosine = jnp.cos(angles)
    sine_part = jnp.sin(angles)
    return (real_part * cosine + imag_part * sine_part, imag_part * cosine - real_part * sine_part)


def turn_back(real_part, imag_part, angles):
    cosine = jnp.cos(angles)
    sine_part = jnp.sin(angles)
    return (real_part * cosine - imag_part * sine_part, imag_part * cosine + real_part * sine_part)


def first_pass(blocks, position, peer_count):
    height, length = blocks.shape
    piece_len = length // peer_count
    padded = 2 * peer_count * length
    shaped = blocks.reshape(height, peer_count, piece_len)
    angles = phases(indices(peer_count), indices(2 * peer_count), 2 * peer_count)
    real_part = product("rdm,dk->rmk", shaped, jnp.cos(angles))
    imag_part = -product("rdm,dk->rmk", shaped, jnp.sin(angles))
    offsets = position * piece_len + indices(piece_len)
    real_part, imag_part = turn_forward(
        real_part, imag_part, phases(offsets, indices(2 * peer_count), padded)
    )
    return jnp.stack([real_part, imag_part])


def second_pass(columns, peer_count):
    height, piece_len = (columns.shape[1], columns.shape[2])
    length = piece_len * peer_count
    real_part = columns[0].reshape(height, piece_len, peer_count, 2)
    imag_part = columns[1].reshape(height, piece_len, peer_count, 2)
    angles = phases(indices(peer_count), indices(peer_count), peer_count)
    cosine = jnp.cos(angles)
    sine_part = jnp.sin(angles)
    real_one = product("rmeb,ea->rbma", real_part, cosine) + product(
        "rmeb,ea->rbma", imag_part, sine_part
    )
    imag_one = product("rmeb,ea->rbma", imag_part, cosine) - product(
        "rmeb,ea->rbma", real_part, sine_part
    )
    real_one, imag_one = turn_forward(
        real_one, imag_one, phases(indices(piece_len), indices(peer_count), length)
    )
    angles = phases(indices(piece_len), indices(piece_len), piece_len)
    cosine = jnp.cos(angles)
    sine_part = jnp.sin(angles)
    real_two = product("rbma,mc->rbca", real_one, cosine) + product(
        "rbma,mc->rbca", imag_one, sine_part
    )
    imag_two = product("rbma,mc->rbca", imag_one, cosine) - product(
        "rbma,mc->rbca", real_one, sine_part
    )
    return jnp.stack([real_two.reshape(height, 2, length), imag_two.reshape(height, 2, length)])


def inverse_first(spectrum, position, peer_count):
    height, length = (spectrum.shape[1], spectrum.shape[3])
    piece_len = length // peer_count
    padded = 2 * peer_count * length
    real_part = spectrum[0].reshape(height, 2, piece_len, peer_count)
    imag_part = spectrum[1].reshape(height, 2, piece_len, peer_count)
    angles = phases(indices(piece_len), indices(piece_len), piece_len)
    cosine = jnp.cos(angles)
    sine_part = jnp.sin(angles)
    real_one = product("rbca,cm->rbma", real_part, cosine) - product(
        "rbca,cm->rbma", imag_part, sine_part
    )
    imag_one = product("rbca,cm->rbma", imag_part, cosine) + product(
        "rbca,cm->rbma", real_part, sine_part
    )
    real_one, imag_one = turn_back(
        real_one, imag_one, phases(indices(piece_len), indices(peer_count), length)
    )
    angles = phases(indices(peer_count), indices(peer_count), peer_count)
    cosine = jnp.cos(angles)
    sine_part = jnp.sin(angles)
    real_two = product("rbma,ae->rmeb", real_one, cosine) - product(
        "rbma,ae->rmeb", imag_one, sine_part
    )
    imag_two = product("rbma,ae->rmeb", imag_one, cosine) + product(
        "rbma,ae->rmeb", real_one, sine_part
    )
    offsets = (indices(peer_count)[None, :] * piece_len + indices(piece_len)[:, None]).reshape(-1)
    freq_bins = 2 * position + indices(2)
    angles = phases(offsets, freq_bins, padded).reshape(piece_len, peer_count, 2)
    real_two, imag_two = turn_back(real_two, imag_two, angles)
    return jnp.stack(
        [
            real_two.reshape(height, piece_len, 2 * peer_count),
            imag_two.reshape(height, piece_len, 2 * peer_count),
        ]
    )


def inverse_second(received, peer_count):
    height, piece_len = (received.shape[1], received.shape[2])
    length = piece_len * peer_count
    padded = 2 * peer_count * length
    angles = phases(indices(2 * peer_count), indices(peer_count), 2 * peer_count)
    signal_out = product("rmk,kd->rdm", received[0], jnp.cos(angles)) - product(
        "rmk,kd->rdm", received[1], jnp.sin(angles)
    )
    return (signal_out / padded).reshape(height, length)


def per_device(signal, gating, cotangent, filters, skip_weight):
    peer_count = lax.axis_size("ctx")
    position = lax.axis_index("ctx")
    channels, length = signal.shape
    count_filters = filters.shape[0]
    local_group = channels // count_filters
    gated_grad = (cotangent.astype(jnp.float32) * gating.astype(jnp.float32)).astype(jnp.bfloat16)
    signal_blocks, gated_blocks = (
        lax.all_to_all(signal, "ctx", split_axis=1, concat_axis=1, tiled=True),
        lax.all_to_all(gated_grad, "ctx", split_axis=1, concat_axis=1, tiled=True),
    )
    tap_blocks = lax.all_to_all(filters, "ctx", split_axis=1, concat_axis=1, tiled=True)
    signal_cols, gated_cols, tap_cols = (
        lax.all_to_all(
            first_pass(signal_blocks.astype(jnp.float32), position, peer_count),
            "ctx",
            split_axis=3,
            concat_axis=3,
            tiled=True,
        ),
        lax.all_to_all(
            first_pass(gated_blocks.astype(jnp.float32), position, peer_count),
            "ctx",
            split_axis=3,
            concat_axis=3,
            tiled=True,
        ),
        lax.all_to_all(
            first_pass(tap_blocks, position, peer_count),
            "ctx",
            split_axis=3,
            concat_axis=3,
            tiled=True,
        ),
    )
    signal_spec = second_pass(signal_cols, peer_count).reshape(
        2, local_group, count_filters, 2, length
    )
    gated_spec = second_pass(gated_cols, peer_count).reshape(
        2, local_group, count_filters, 2, length
    )
    tap_spec = second_pass(tap_cols, peer_count)
    tap_real, tap_imag = (tap_spec[0], tap_spec[1])
    sig_real, sig_imag = (signal_spec[0], signal_spec[1])
    gated_real, gated_imag = (gated_spec[0], gated_spec[1])
    forward_spec = jnp.stack(
        [sig_real * tap_real - sig_imag * tap_imag, sig_real * tap_imag + sig_imag * tap_real]
    ).reshape(2, channels, 2, length)
    back_spec = jnp.stack(
        [
            tap_real * gated_real + tap_imag * gated_imag,
            tap_real * gated_imag - tap_imag * gated_real,
        ]
    ).reshape(2, channels, 2, length)
    corr_spec = jnp.stack(
        [
            jnp.sum(sig_real * gated_real + sig_imag * gated_imag, axis=0),
            jnp.sum(sig_real * gated_imag - sig_imag * gated_real, axis=0),
        ]
    )
    forward_cols, back_cols, corr_cols = (
        lax.all_to_all(
            inverse_first(forward_spec, position, peer_count),
            "ctx",
            split_axis=3,
            concat_axis=3,
            tiled=True,
        ),
        lax.all_to_all(
            inverse_first(back_spec, position, peer_count),
            "ctx",
            split_axis=3,
            concat_axis=3,
            tiled=True,
        ),
        lax.all_to_all(
            inverse_first(corr_spec, position, peer_count),
            "ctx",
            split_axis=3,
            concat_axis=3,
            tiled=True,
        ),
    )
    conv_time, back_time, corr_time = (
        lax.all_to_all(
            inverse_second(forward_cols, peer_count), "ctx", split_axis=1, concat_axis=1, tiled=True
        ),
        lax.all_to_all(
            inverse_second(back_cols, peer_count), "ctx", split_axis=1, concat_axis=1, tiled=True
        ),
        lax.all_to_all(
            inverse_second(corr_cols, peer_count), "ctx", split_axis=1, concat_axis=1, tiled=True
        ),
    )
    corr_time = lax.psum_scatter(corr_time, "chan", scatter_dimension=0, tiled=True)
    weight = skip_weight[:, None]
    outputs = conv_time + weight * signal.astype(jnp.float32)
    grad_gating = (cotangent.astype(jnp.float32) * outputs).astype(jnp.bfloat16)
    grad_signal = (back_time + weight * gated_grad.astype(jnp.float32)).astype(jnp.bfloat16)
    normal_scale = 1.0 / math.sqrt(length * peer_count * local_group * lax.axis_size("chan"))
    grad_filters = corr_time * normal_scale
    return (grad_signal, grad_gating, grad_filters)


def solution(mesh):
    in_specs = (P("chan", "ctx"), P("chan", "ctx"), P("chan", "ctx"), P(None, "ctx"), P("chan"))
    out_specs = (P("chan", "ctx"), P("chan", "ctx"), P("chan", "ctx"))
    return jax.shard_map(
        per_device, mesh=mesh, in_specs=in_specs, out_specs=out_specs, check_vma=False
    )
```

profile of v0, /device:TPU:0, one launch (start us, length us, event | category | flops | bytes accessed | tf_op | source)
XLA Modules:
  0.0 228.4 jit_solution(14826324804093838601)
XLA Ops:
  7.2 1.5 copy_bitcast_fusion.14
  8.7 7.3 %all-to-all-start.6 = ((bf16[32,8,128]{2,0,1:T(8,128)(2,1)}), bf16[32,8,128]{2,0,1:T(8,128)(2,1)S(1)}, u32[]{:S(2)}, u32[]{:S(2)}) async-start(bf16[32,8,128]{2,0,1:T(8,128)(2,1)} %copy_bitcast_fusion.14), calls=%async_computation.6 | async-start | bytes 131072 | tf_op jit(solution)/shard_map/all_to_all | solution.py:138
  17.6 5.3 %all-to-all-done.6 = bf16[32,8,128]{2,0,1:T(8,128)(2,1)S(1)} async-done(((bf16[32,8,128]{2,0,1:T(8,128)(2,1)}), bf16[32,8,128]{2,0,1:T(8,128)(2,1)S(1)}, u32[]{:S(2)}, u32[]{:S(2)}) %all-to-all-start.6) | async-done | bytes 65568 | tf_op jit(solution)/shard_map/all_to_all | solution.py:138
  22.9 3.4 %all-to-all-start.2 = ((bf16[32,8,128]{2,0,1:T(8,128)(2,1)}), bf16[32,8,128]{2,0,1:T(8,128)(2,1)S(1)}, u32[]{:S(2)}, u32[]{:S(2)}) async-start(bf16[32,8,128]{2,0,1:T(8,128)(2,1)} %copy_bitcast_fusion.15), calls=%async_computation.2 | async-start | bytes 131072 | tf_op jit(solution)/shard_map/all_to_all | solution.py:139
  27.0 6.1 %all-to-all-done.2 = bf16[32,8,128]{2,0,1:T(8,128)(2,1)S(1)} async-done(((bf16[32,8,128]{2,0,1:T(8,128)(2,1)}), bf16[32,8,128]{2,0,1:T(8,128)(2,1)S(1)}, u32[]{:S(2)}, u32[]{:S(2)}) %all-to-all-start.2) | async-done | bytes 65568 | tf_op jit(solution)/shard_map/all_to_all | solution.py:139
  33.1 3.4 %all-to-all-start = ((f32[32,8,128]{2,0,1:T(8,128)}), f32[32,8,128]{2,0,1:T(8,128)S(1)}, u32[]{:S(2)}, u32[]{:S(2)}) async-start(f32[32,8,128]{2,0,1:T(8,128)} %copy_bitcast_fusion.13), calls=%async_computation | async-start | bytes 262144 | tf_op jit(solution)/shard_map/all_to_all | solution.py:141
  37.2 6.5 %all-to-all-done = f32[32,8,128]{2,0,1:T(8,128)S(1)} async-done(((f32[32,8,128]{2,0,1:T(8,128)}), f32[32,8,128]{2,0,1:T(8,128)S(1)}, u32[]{:S(2)}, u32[]{:S(2)}) %all-to-all-start) | async-done | bytes 131104 | tf_op jit(solution)/shard_map/all_to_all | solution.py:141
  44.8 1.0 copy.146
  45.8 3.5 %all-to-all-start.1 = ((f32[2,32,128,16]{2,1,0,3:T(8,128)}), f32[2,32,128,16]{2,1,0,3:T(8,128)S(1)}, u32[]{:S(2)}, u32[]{:S(2)}) async-start(f32[2,32,128,16]{2,1,0,3:T(8,128)} %copy.146), calls=%async_computation.1 | async-start | bytes 1048576 | tf_op jit(solution)/shard_map/all_to_all | solution.py:157
  49.6 1.0 copy.158
  50.6 1.0 copy.185
  51.6 8.7 %all-to-all-done.1 = f32[2,32,128,16]{2,1,0,3:T(8,128)S(1)} async-done(((f32[2,32,128,16]{2,1,0,3:T(8,128)}), f32[2,32,128,16]{2,1,0,3:T(8,128)S(1)}, u32[]{:S(2)}, u32[]{:S(2)}) %all-to-all-start.1) | async-done | bytes 524320 | tf_op jit(solution)/shard_map/all_to_all | solution.py:157
  60.3 3.7 %all-to-all-start.3 = ((f32[2,32,128,16]{2,1,0,3:T(8,128)}), f32[2,32,128,16]{2,1,0,3:T(8,128)S(1)}, u32[]{:S(2)}, u32[]{:S(2)}) async-start(f32[2,32,128,16]{2,1,0,3:T(8,128)} %copy.158), calls=%async_computation.3 | async-start | bytes 1048576 | tf_op jit(solution)/shard_map/all_to_all | solution.py:150
  65.5 10.9 %all-to-all-done.3 = f32[2,32,128,16]{2,1,0,3:T(8,128)S(1)} async-done(((f32[2,32,128,16]{2,1,0,3:T(8,128)}), f32[2,32,128,16]{2,1,0,3:T(8,128)S(1)}, u32[]{:S(2)}, u32[]{:S(2)}) %all-to-all-start.3) | async-done | bytes 524320 | tf_op jit(solution)/shard_map/all_to_all | solution.py:150
  76.4 3.7 %all-to-all-start.7 = ((f32[2,32,128,16]{2,1,0,3:T(8,128)}), f32[2,32,128,16]{2,1,0,3:T(8,128)S(1)}, u32[]{:S(2)}, u32[]{:S(2)}) async-start(f32[2,32,128,16]{2,1,0,3:T(8,128)} %copy.185), calls=%async_computation.7 | async-start | bytes 1048576 | tf_op jit(solution)/shard_map/all_to_all | solution.py:143
  82.6 10.8 %all-to-all-done.7 = f32[2,32,128,16]{2,1,0,3:T(8,128)S(1)} async-done(((f32[2,32,128,16]{2,1,0,3:T(8,128)}), f32[2,32,128,16]{2,1,0,3:T(8,128)S(1)}, u32[]{:S(2)}, u32[]{:S(2)}) %all-to-all-start.7) | async-done | bytes 524320 | tf_op jit(solution)/shard_map/all_to_all | solution.py:143
  103.2 0.9 fusion.33
  116.6 0.9 multiply_subtract_fusion
  118.6 3.7 %all-to-all-start.10 = ((f32[2,32,128,16]{2,1,0,3:T(8,128)}), f32[2,32,128,16]{2,1,0,3:T(8,128)S(1)}, u32[]{:S(2)}, u32[]{:S(2)}) async-start(f32[2,32,128,16]{2,1,0,3:T(8,128)} %copy.213), calls=%async_computation.10 | async-start | bytes 1048576 | tf_op jit(solution)/shard_map/all_to_all | solution.py:205
  123.3 12.7 %all-to-all-done.10 = f32[2,32,128,16]{2,1,0,3:T(8,128)S(1)} async-done(((f32[2,32,128,16]{2,1,0,3:T(8,128)}), f32[2,32,128,16]{2,1,0,3:T(8,128)S(1)}, u32[]{:S(2)}, u32[]{:S(2)}) %all-to-all-start.10) | async-done | bytes 524320 | tf_op jit(solution)/shard_map/all_to_all | solution.py:205
  136.0 3.6 %all-to-all-start.8 = ((f32[2,32,128,16]{2,1,0,3:T(8,128)}), f32[2,32,128,16]{2,1,0,3:T(8,128)S(1)}, u32[]{:S(2)}, u32[]{:S(2)}) async-start(f32[2,32,128,16]{2,1,0,3:T(8,128)} %copy.202), calls=%async_computation.8 | async-start | bytes 1048576 | tf_op jit(solution)/shard_map/all_to_all | solution.py:191
  141.2 12.3 %all-to-all-done.8 = f32[2,32,128,16]{2,1,0,3:T(8,128)S(1)} async-done(((f32[2,32,128,16]{2,1,0,3:T(8,128)}), f32[2,32,128,16]{2,1,0,3:T(8,128)S(1)}, u32[]{:S(2)}, u32[]{:S(2)}) %all-to-all-start.8) | async-done | bytes 524320 | tf_op jit(solution)/shard_map/all_to_all | solution.py:191
  153.5 3.6 %all-to-all-start.4 = ((f32[2,32,128,16]{2,1,0,3:T(8,128)}), f32[2,32,128,16]{2,1,0,3:T(8,128)S(1)}, u32[]{:S(2)}, u32[]{:S(2)}) async-start(f32[2,32,128,16]{2,1,0,3:T(8,128)} %copy.177), calls=%async_computation.4 | async-start | bytes 1048576 | tf_op jit(solution)/shard_map/all_to_all | solution.py:198
  159.8 11.1 %all-to-all-done.4 = f32[2,32,128,16]{2,1,0,3:T(8,128)S(1)} async-done(((f32[2,32,128,16]{2,1,0,3:T(8,128)}), f32[2,32,128,16]{2,1,0,3:T(8,128)S(1)}, u32[]{:S(2)}, u32[]{:S(2)}) %all-to-all-start.4) | async-done | bytes 524320 | tf_op jit(solution)/shard_map/all_to_all | solution.py:198
  170.9 3.6 %all-to-all-start.11 = ((f32[32,8,128]{2,0,1:T(8,128)}), f32[32,8,128]{2,0,1:T(8,128)S(1)}, u32[]{:S(2)}, u32[]{:S(2)}) async-start(f32[32,8,128]{2,0,1:T(8,128)} %copy.216), calls=%async_computation.11 | async-start | bytes 262144 | tf_op jit(solution)/shard_map/all_to_all | solution.py:220
  175.0 6.9 %all-to-all-done.11 = f32[32,8,128]{2,0,1:T(8,128)S(1)} async-done(((f32[32,8,128]{2,0,1:T(8,128)}), f32[32,8,128]{2,0,1:T(8,128)S(1)}, u32[]{:S(2)}, u32[]{:S(2)}) %all-to-all-start.11) | async-done | bytes 131104 | tf_op jit(solution)/shard_map/all_to_all | solution.py:220
  181.9 3.4 %all-to-all-start.9 = ((f32[32,8,128]{2,0,1:T(8,128)}), f32[32,8,128]{2,0,1:T(8,128)S(1)}, u32[]{:S(2)}, u32[]{:S(2)}) async-start(f32[32,8,128]{2,0,1:T(8,128)} %copy.205), calls=%async_computation.9 | async-start | bytes 262144 | tf_op jit(solution)/shard_map/all_to_all | solution.py:214
  186.4 6.2 %all-to-all-done.9 = f32[32,8,128]{2,0,1:T(8,128)S(1)} async-done(((f32[32,8,128]{2,0,1:T(8,128)}), f32[32,8,128]{2,0,1:T(8,128)S(1)}, u32[]{:S(2)}, u32[]{:S(2)}) %all-to-all-start.9) | async-done | bytes 131104 | tf_op jit(solution)/shard_map/all_to_all | solution.py:214
  192.5 3.4 %all-to-all-start.5 = ((f32[32,8,128]{2,0,1:T(8,128)}), f32[32,8,128]{2,0,1:T(8,128)S(1)}, u32[]{:S(2)}, u32[]{:S(2)}) async-start(f32[32,8,128]{2,0,1:T(8,128)} %copy.180), calls=%async_computation.5 | async-start | bytes 262144 | tf_op jit(solution)/shard_map/all_to_all | solution.py:217
  196.7 6.5 %all-to-all-done.5 = f32[32,8,128]{2,0,1:T(8,128)S(1)} async-done(((f32[32,8,128]{2,0,1:T(8,128)}), f32[32,8,128]{2,0,1:T(8,128)S(1)}, u32[]{:S(2)}, u32[]{:S(2)}) %all-to-all-start.5) | async-done | bytes 131104 | tf_op jit(solution)/shard_map/all_to_all | solution.py:217
  204.0 16.2 %reduce-scatter.2.cloned.1.call-done = f32[8,1024]{1,0:T(8,128)} async-done(((f32[32,1024]{1,0:T(8,128)}), f32[8,1024]{1,0:T(8,128)}) %reduce-scatter.2.cloned.1.call-update) | async-done | bytes 32784 | tf_op jit(solution)/shard_map/reduce_scatter | solution.py:224
  220.1 1.4 broadcast_multiply_fusion
  (105 shorter events, 39.8 us)
Async XLA Ops:
  7.2 8.8 %copy-start = (f32[32,1024]{1,0:T(8,128)S(1)}, f32[32,1024]{1,0:T(8,128)}, u32[]{:S(2)}) copy-start(f32[32,1024]{1,0:T(8,128)} %param.8) | copy-start | bytes 393220
  8.7 14.2 %all-to-all-start.6 = ((bf16[32,8,128]{2,0,1:T(8,128)(2,1)}), bf16[32,8,128]{2,0,1:T(8,128)(2,1)S(1)}, u32[]{:S(2)}, u32[]{:S(2)}) async-start(bf16[32,8,128]{2,0,1:T(8,128)(2,1)} %copy_bitcast_fusion.14), calls=%async_computation.6 | async-start | bytes 131072 | tf_op jit(solution)/shard_map/all_to_all | solution.py:138
  16.0 0.8 copy-start.1
  16.0 0.9 copy-start.2
  22.9 10.2 %all-to-all-start.2 = ((bf16[32,8,128]{2,0,1:T(8,128)(2,1)}), bf16[32,8,128]{2,0,1:T(8,128)(2,1)S(1)}, u32[]{:S(2)}, u32[]{:S(2)}) async-start(bf16[32,8,128]{2,0,1:T(8,128)(2,1)} %copy_bitcast_fusion.15), calls=%async_computation.2 | async-start | bytes 131072 | tf_op jit(solution)/shard_map/all_to_all | solution.py:139
  33.1 10.7 %all-to-all-start = ((f32[32,8,128]{2,0,1:T(8,128)}), f32[32,8,128]{2,0,1:T(8,128)S(1)}, u32[]{:S(2)}, u32[]{:S(2)}) async-start(f32[32,8,128]{2,0,1:T(8,128)} %copy_bitcast_fusion.13), calls=%async_computation | async-start | bytes 262144 | tf_op jit(solution)/shard_map/all_to_all | solution.py:141
  45.8 14.5 %all-to-all-start.1 = ((f32[2,32,128,16]{2,1,0,3:T(8,128)}), f32[2,32,128,16]{2,1,0,3:T(8,128)S(1)}, u32[]{:S(2)}, u32[]{:S(2)}) async-start(f32[2,32,128,16]{2,1,0,3:T(8,128)} %copy.146), calls=%async_computation.1 | async-start | bytes 1048576 | tf_op jit(solution)/shard_map/all_to_all | solution.py:157
  60.3 16.1 %all-to-all-start.3 = ((f32[2,32,128,16]{2,1,0,3:T(8,128)}), f32[2,32,128,16]{2,1,0,3:T(8,128)S(1)}, u32[]{:S(2)}, u32[]{:S(2)}) async-start(f32[2,32,128,16]{2,1,0,3:T(8,128)} %copy.158), calls=%async_computation.3 | async-start | bytes 1048576 | tf_op jit(solution)/shard_map/all_to_all | solution.py:150
  76.4 17.0 %all-to-all-start.7 = ((f32[2,32,128,16]{2,1,0,3:T(8,128)}), f32[2,32,128,16]{2,1,0,3:T(8,128)S(1)}, u32[]{:S(2)}, u32[]{:S(2)}) async-start(f32[2,32,128,16]{2,1,0,3:T(8,128)} %copy.185), calls=%async_computation.7 | async-start | bytes 1048576 | tf_op jit(solution)/shard_map/all_to_all | solution.py:143
  118.6 17.5 %all-to-all-start.10 = ((f32[2,32,128,16]{2,1,0,3:T(8,128)}), f32[2,32,128,16]{2,1,0,3:T(8,128)S(1)}, u32[]{:S(2)}, u32[]{:S(2)}) async-start(f32[2,32,128,16]{2,1,0,3:T(8,128)} %copy.213), calls=%async_computation.10 | async-start | bytes 1048576 | tf_op jit(solution)/shard_map/all_to_all | solution.py:205
  136.0 17.4 %all-to-all-start.8 = ((f32[2,32,128,16]{2,1,0,3:T(8,128)}), f32[2,32,128,16]{2,1,0,3:T(8,128)S(1)}, u32[]{:S(2)}, u32[]{:S(2)}) async-start(f32[2,32,128,16]{2,1,0,3:T(8,128)} %copy.202), calls=%async_computation.8 | async-start | bytes 1048576 | tf_op jit(solution)/shard_map/all_to_all | solution.py:191
  153.5 17.4 %all-to-all-start.4 = ((f32[2,32,128,16]{2,1,0,3:T(8,128)}), f32[2,32,128,16]{2,1,0,3:T(8,128)S(1)}, u32[]{:S(2)}, u32[]{:S(2)}) async-start(f32[2,32,128,16]{2,1,0,3:T(8,128)} %copy.177), calls=%async_computation.4 | async-start | bytes 1048576 | tf_op jit(solution)/shard_map/all_to_all | solution.py:198
  170.9 11.0 %all-to-all-start.11 = ((f32[32,8,128]{2,0,1:T(8,128)}), f32[32,8,128]{2,0,1:T(8,128)S(1)}, u32[]{:S(2)}, u32[]{:S(2)}) async-start(f32[32,8,128]{2,0,1:T(8,128)} %copy.216), calls=%async_computation.11 | async-start | bytes 262144 | tf_op jit(solution)/shard_map/all_to_all | solution.py:220
  181.9 10.7 %all-to-all-start.9 = ((f32[32,8,128]{2,0,1:T(8,128)}), f32[32,8,128]{2,0,1:T(8,128)S(1)}, u32[]{:S(2)}, u32[]{:S(2)}) async-start(f32[32,8,128]{2,0,1:T(8,128)} %copy.205), calls=%async_computation.9 | async-start | bytes 262144 | tf_op jit(solution)/shard_map/all_to_all | solution.py:214
  192.5 10.7 %all-to-all-start.5 = ((f32[32,8,128]{2,0,1:T(8,128)}), f32[32,8,128]{2,0,1:T(8,128)S(1)}, u32[]{:S(2)}, u32[]{:S(2)}) async-start(f32[32,8,128]{2,0,1:T(8,128)} %copy.180), calls=%async_computation.5 | async-start | bytes 262144 | tf_op jit(solution)/shard_map/all_to_all | solution.py:217
  195.9 24.2 %reduce-scatter.2.cloned.1.call-start = ((), (), s32[]{:S(2)}) async-start(), calls=%async_computation.13 | async-start | bytes 163840 | tf_op jit(solution)/shard_map/reduce_scatter | solution.py:224
  196.6 6.6 %copy-start.3 = (bf16[32,1024]{1,0:T(8,128)(2,1)S(1)}, bf16[32,1024]{1,0:T(8,128)(2,1)}, u32[]{:S(2)}) copy-start(bf16[32,1024]{1,0:T(8,128)(2,1)} %param.5) | copy-start | bytes 196612
  196.6 6.6 %copy-start.4 = (f32[32]{0:T(128)S(1)}, f32[32]{0:T(128)}, u32[]{:S(2)}) copy-start(f32[32]{0:T(128)} %param.9) | copy-start | bytes 388
Sparse Core Ops, SparseCore 0:
  199.2 20.9 reduce-scatter.1
where the time goes:
time: 230 us; the launch traced here: 228 us
  waiting for transfers between devices  120 us (52%)
  starting transfers between devices  46.2 us (20%)
  matrix products  32.7 us (14%)
  between operations  14.7 us (6%)
  local copies, waits for them, and re-layouts  11.3 us (5%)
  other arithmetic  3.32 us (1%)
    dot_general x60, matrix products, product(): jnp.einsum(form, left, right, precision=lax.Precision.HIGHEST, preferred_...  32.7 us
    reduce_scatter x1, waiting for transfers between devices, per_device(): lax.psum_scatter(corr_time, 'chan', scatter_dimension=0, tiled=True)  16.2 us
    all_to_all x1, waiting for transfers between devices, per_device(): lax.all_to_all(inverse_first(corr_spec, position, peer_count), 'ctx', spl...  12.7 us
    all_to_all x1, waiting for transfers between devices, per_device(): lax.all_to_all(inverse_first(forward_spec, position, peer_count), 'ctx',...  12.3 us
    all_to_all x1, waiting for transfers between devices, per_device(): lax.all_to_all(inverse_first(back_spec, position, peer_count), 'ctx', spl...  11.1 us
    all_to_all x1, waiting for transfers between devices, per_device(): lax.all_to_all(first_pass(gated_blocks.astype(jnp.float32), position, pee...  10.9 us
    all_to_all x1, waiting for transfers between devices, per_device(): lax.all_to_all(first_pass(signal_blocks.astype(jnp.float32), position, pe...  10.8 us
    all_to_all x1, waiting for transfers between devices, per_device(): lax.all_to_all(first_pass(tap_blocks, position, peer_count), 'ctx', split...  8.67 us
  transfers between devices with their start and end apart: 13, of which 13 were waited for; matrix products, arithmetic and copies ran while one was open for 8% of the time, Pallas kernels for 0%

commit v1 on v0

--- a/solution.py
+++ b/solution.py
@@ -1,9 +1,182 @@
+import functools
 import math
 
 import jax
 import jax.numpy as jnp
+import numpy as np
 from jax import lax
+from jax.experimental import pallas as pl
+from jax.experimental.pallas import tpu as pltpu
 from jax.sharding import PartitionSpec as P
+
+LANES = 128
+
+
+def split_table(table):
+    high = table.astype(jnp.bfloat16)
+    low = (table - high.astype(np.float64)).astype(jnp.bfloat16)
+    return high, low
+
+
+def dft_tables(rows):
+    height = 2 * rows
+    padded = height * LANES
+    kept = rows + 1
+    pad = -kept % 16
+    k1 = np.arange(kept)
+    n1 = np.arange(rows)
+    n2 = np.arange(LANES)
+    zeros = lambda table, axis: np.pad(table, [(0, pad if a == axis else 0) for a in range(2)])
+    outer = 2.0 * np.pi * (np.outer(k1, n1) % height) / height
+    first = np.concatenate([zeros(np.cos(outer), 0), zeros(-np.sin(outer), 0)], axis=0)
+    high, low = split_table(first)
+    first = np.concatenate([high, low, high, low], axis=1)
+    turn = 2.0 * np.pi * (np.outer(k1, n2) % padded) / padded
+    twiddle = np.stack([zeros(np.cos(turn), 0), zeros(np.sin(turn), 0)]).astype(np.float32)
+    inner = 2.0 * np.pi * (np.outer(n2, n2) % LANES) / LANES
+    cosine, sine = np.cos(inner), np.sin(inner)
+    second = np.stack(split_table(np.block([[cosine, -sine], [sine, cosine]])))
+    weight = np.where((k1 == 0) | (k1 == rows), 1.0, 2.0) / padded
+    last = np.concatenate(
+        [zeros(np.cos(outer.T) * weight, 1), zeros(-np.sin(outer.T) * weight, 1)], axis=1
+    )
+    last = np.concatenate(split_table(last), axis=0)
+    return first, twiddle, second, last
+
+
+def dot(left, right):
+    return jnp.dot(left, right, preferred_element_type=jnp.float32)
+
+
+def split(values):
+    high = values.astype(jnp.bfloat16)
+    return high, (values - high.astype(jnp.float32)).astype(jnp.bfloat16)
+
+
+def spectral_kernel(
+    groups, peers, scale, got_ref, first_ref, twiddle_ref, second_ref, last_ref, out_ref, in_ref, part_ref, spec_ref, back_ref
+):
+    piece = got_ref.shape[1] // 3
+    taps = piece // groups
+    rows = peers * piece
+    kept = twiddle_ref.shape[1]
+    count = 2 * groups
+    got = [got_ref[source].astype(jnp.float32) for source in range(peers * groups)]
+
+    def gather(group, start):
+        parts = [got[peer * groups + group][start : start + piece] for peer in range(peers)]
+        return jnp.concatenate(parts, axis=0).astype(jnp.bfloat16)
+
+    for sequence in range(count):
+        group, start = sequence % groups, sequence // groups * piece
+        values = gather(group, start)
+        in_ref[0:rows, sequence * LANES : (sequence + 1) * LANES] = values
+        in_ref[rows : 2 * rows, sequence * LANES : (sequence + 1) * LANES] = values
+    tap_high = jnp.concatenate([part[2 * piece : 2 * piece + taps] for part in got], axis=0).astype(jnp.bfloat16)
+    tap_low = jnp.concatenate([part[2 * piece + taps : 2 * piece + 2 * taps] for part in got], axis=0).astype(jnp.bfloat16)
+    tap_in = jnp.concatenate([tap_high, tap_high, tap_low, tap_low], axis=0)
+    cosine, sine = twiddle_ref[0], twiddle_ref[1]
+    stage = dot(first_ref[:, : 2 * rows], in_ref[...])
+    tap_stage = dot(first_ref[...], tap_in)
+    total = (count + 1) * kept
+    for sequence in range(count + 1):
+        source = tap_stage if sequence == count else stage[:, sequence * LANES : (sequence + 1) * LANES]
+        real, imag = source[:kept], source[kept:]
+        turned = jnp.concatenate([real * cosine + imag * sine, imag * cosine - real * sine], axis=1)
+        high, low = split(turned)
+        part_ref[sequence * kept : (sequence + 1) * kept] = high
+        part_ref[total + sequence * kept : total + (sequence + 1) * kept] = low
+
+    def second_stage():
+        both = dot(part_ref[...], second_ref[0])
+        spec_ref[...] = both[:total] + both[total:] + dot(part_ref[:total], second_ref[1])
+
+    second_stage()
+    tap = spec_ref[count * kept : total]
+    tap_real, tap_imag = tap[:, :LANES], tap[:, LANES:]
+    corr_real = corr_imag = None
+
+    def put(sequence, real, imag):
+        high, low = split(jnp.concatenate([imag, real], axis=1))
+        part_ref[sequence * kept : (sequence + 1) * kept] = high
+        part_ref[total + sequence * kept : total + (sequence + 1) * kept] = low
+
+    for group in range(groups):
+        sig = spec_ref[group * kept : (group + 1) * kept]
+        gat = spec_ref[(groups + group) * kept : (groups + group + 1) * kept]
+        sr, si, gr, gi = sig[:, :LANES], sig[:, LANES:], gat[:, :LANES], gat[:, LANES:]
+        put(group, sr * tap_real - si * tap_imag, sr * tap_imag + si * tap_real)
+        put(groups + group, tap_real * gr + tap_imag * gi, tap_real * gi - tap_imag * gr)
+        cr, ci = sr * gr + si * gi, sr * gi - si * gr
+        corr_real, corr_imag = (cr, ci) if corr_real is None else (corr_real + cr, corr_imag + ci)
+    put(count, corr_real * scale, corr_imag * scale)
+    second_stage()
+    for sequence in range(count + 1):
+        both = spec_ref[sequence * kept : (sequence + 1) * kept]
+        imag, real = both[:, :LANES], both[:, LANES:]
+        turned = jnp.concatenate([real * cosine - imag * sine, imag * cosine + real * sine], axis=0)
+        high, low = split(turned)
+        back_ref[0, :, sequence * LANES : (sequence + 1) * LANES] = high
+        back_ref[1, :, sequence * LANES : (sequence + 1) * LANES] = low
+    both = dot(last_ref[...], back_ref[0])
+    result = both[:rows] + both[rows:] + dot(last_ref[:rows], back_ref[1])
+    for peer in range(peers):
+        piece_rows = result[peer * piece : (peer + 1) * piece]
+        for group in range(groups):
+            cut = lambda sequence: piece_rows[:, sequence * LANES : (sequence + 1) * LANES]
+            message = jnp.concatenate([cut(group), cut(groups + group), cut(count)], axis=0)
+            out_ref[peer * groups + group] = message.astype(jnp.bfloat16)
+
+
+def spectral_products(got, groups, peers, scale):
+    rows = peers * (got.shape[1] // 3)
+    tables = dft_tables(rows)
+    kept = tables[1].shape[1]
+    total = (2 * groups + 1) * kept
+    vmem = pl.BlockSpec(memory_space=pltpu.VMEM)
+    return pl.pallas_call(
+        functools.partial(spectral_kernel, groups, peers, scale),
+        out_shape=jax.ShapeDtypeStruct(got.shape, jnp.bfloat16),
+        in_specs=[vmem] * 5,
+        out_specs=vmem,
+        scratch_shapes=[
+            pltpu.VMEM((2 * rows, 2 * groups * LANES), jnp.bfloat16),
+            pltpu.VMEM((2 * total, 2 * LANES), jnp.bfloat16),
+            pltpu.VMEM((total, 2 * LANES), jnp.float32),
+            pltpu.VMEM((2, 2 * kept, (2 * groups + 1) * LANES), jnp.bfloat16),
+        ],
+        compiler_params=pltpu.CompilerParams(vmem_limit_bytes=40 * 2**20),
+        name="spectral_products",
+    )(got, *[jnp.asarray(table) for table in tables])
+
+
+def filter_per_device(signal, gating, cotangent, filters, skip_weight):
+    peers = lax.axis_size("ctx")
+    groups = lax.axis_size("chan")
+    channels, length = signal.shape
+    piece = length // LANES
+    taps = piece // groups
+    both_axes = ("ctx", "chan")
+    gated_grad = (cotangent.astype(jnp.float32) * gating.astype(jnp.float32)).astype(jnp.bfloat16)
+    own = lax.dynamic_slice_in_dim(filters, lax.axis_index("chan") * (length // groups), length // groups, axis=1)
+    tap_high = own.astype(jnp.bfloat16)
+    tap_low = (own - tap_high.astype(jnp.float32)).astype(jnp.bfloat16)
+    tiles = lambda array: array.reshape(channels, -1, LANES)
+    message = jnp.concatenate([tiles(signal), tiles(gated_grad), tiles(tap_high), tiles(tap_low)], axis=1)
+    message = jnp.pad(message, ((0, 0), (0, 3 * piece - message.shape[1]), (0, 0)))
+    got = lax.all_to_all(message, both_axes, split_axis=0, concat_axis=0, tiled=True)
+    scale = 1.0 / math.sqrt(length * peers * groups)
+    result = spectral_products(got, groups, peers, scale)
+    home = lax.all_to_all(result, both_axes, split_axis=0, concat_axis=0, tiled=True).astype(jnp.float32)
+    conv = home[:, :piece].reshape(channels, length)
+    back = home[:, piece : 2 * piece].reshape(channels, length)
+    weight = skip_weight[:, None]
+    outputs = conv + weight * signal.astype(jnp.float32)
+    grad_gating = (cotangent.astype(jnp.float32) * outputs).astype(jnp.bfloat16)
+    grad_signal = (back + weight * gated_grad.astype(jnp.float32)).astype(jnp.bfloat16)
+    share = channels // groups
+    corr = lax.dynamic_slice_in_dim(home[:, 2 * piece :], lax.axis_index("chan") * share, share, axis=0)
+    return (grad_signal, grad_gating, corr.reshape(share, length))
 
 
 def product(form, left, right):
@@ -127,7 +300,7 @@
     return (signal_out / padded).reshape(height, length)
 
 
-def per_device(signal, gating, cotangent, filters, skip_weight):
+def split_transforms(signal, gating, cotangent, filters, skip_weight):
     peer_count = lax.axis_size("ctx")
     position = lax.axis_index("ctx")
     channels, length = signal.shape
@@ -231,6 +404,16 @@
     return (grad_signal, grad_gating, grad_filters)
 
 
+def per_device(signal, gating, cotangent, filters, skip_weight):
+    peers, groups = lax.axis_size("ctx"), lax.axis_size("chan")
+    channels, length = signal.shape
+    one_each = channels == filters.shape[0] == peers * groups
+    whole_tiles = length % (8 * LANES) == 0 and (length // LANES) % groups == 0
+    if one_each and whole_tiles and 2 * (length // LANES // groups) <= length // LANES:
+        return filter_per_device(signal, gating, cotangent, filters, skip_weight)
+    return split_transforms(signal, gating, cotangent, filters, skip_weight)
+
+
 def solution(mesh):
     in_specs = (P("chan", "ctx"), P("chan", "ctx"), P("chan", "ctx"), P(None, "ctx"), P("chan"))
     out_specs = (P("chan", "ctx"), P("chan", "ctx"), P("chan", "ctx"))

time: 230 us -> 35.2 us (0.15)
  waiting for transfers between devices: 120 us -> 8.89 us
  starting transfers between devices: 46.2 us -> 2.72 us
  matrix products: 32.7 us -> 0 us
  blocking collectives: 0 us -> 16 us
  between operations: 14.7 us -> 0.76 us
  local copies, waits for them, and re-layouts: 11.3 us -> 2.24 us
  Pallas kernels: 0 us -> 2.48 us
    all_to_all x12 -> x1, waiting for transfers between devices: 104 us -> 8.89 us  [filter_per_device(): lax.all_to_all(result, both_axes, split_axis=0, concat_axis=0, tiled=True)]
    all_to_all x12 -> x1, starting transfers between devices: 46.2 us -> 2.72 us  [filter_per_device(): lax.all_to_all(result, both_axes, split_axis=0, concat_axis=0, tiled=True)]
    dot_general x60 -> x0, matrix products: 32.7 us -> none  [product(): jnp.einsum(form, left, right, precision=lax.Precision.HIGHEST, preferred_...]
    reduce_scatter x1 -> x0, waiting for transfers between devices: 16.2 us -> none  [per_device(): lax.psum_scatter(corr_time, 'chan', scatter_dimension=0, tiled=True)]
    all_to_all x0 -> x1, blocking collectives: none -> 16 us  [filter_per_device(): lax.all_to_all(message, both_axes, split_axis=0, concat_axis=0, tiled=True)]
    another operation x6 -> x0, local copies, waits for them, and re-layouts: 5.44 us -> none  [the longest x3 2.91 us: first_pass(): return jnp.stack([real_part, imag_part])]
    all_to_all x3 -> x0, local copies, waits for them, and re-layouts: 2.84 us -> none  [the longest x1 1.52 us: per_device(): lax.all_to_all(signal, 'ctx', split_axis=1, concat_axis=1, tiled=True)]
    pallas_call x0 -> x1, Pallas kernels: none -> 2.48 us  [spectral_products(): pl.pallas_call(functools.partial(spectral_kernel, groups, peers, scale),...]
  transfers between devices with their start and end apart: 13 -> 1, of which waited for: 13 -> 1; matrix products, arithmetic and copies ran while one was open for 8% -> 0% of each run, Pallas kernels for 0% -> 0%
where the time goes in v1:
time: 35.2 us; the launch traced here: 34.8 us
  blocking collectives  16 us (45%)
  waiting for transfers between devices  8.89 us (25%)
  starting transfers between devices  2.72 us (8%)
  Pallas kernels  2.48 us (7%)
  local copies, waits for them, and re-layouts  2.24 us (6%)
  other arithmetic  1.72 us (5%)
  between operations  0.76 us (2%)
    all_to_all x1, blocking collectives, filter_per_device(): lax.all_to_all(message, both_axes, split_axis=0, concat_axis=0, tiled=True)  16 us
    all_to_all x1, waiting for transfers between devices, filter_per_device(): lax.all_to_all(result, both_axes, split_axis=0, concat_axis=0, tiled=True)  8.89 us
    all_to_all x1, starting transfers between devices, filter_per_device(): lax.all_to_all(result, both_axes, split_axis=0, concat_axis=0, tiled=True)  2.72 us
    pallas_call x1, Pallas kernels, spectral_products(): pl.pallas_call(functools.partial(spectral_kernel, groups, peers, scale),...  2.48 us
    unnamed x20, local copies, waits for them, and re-layouts  2.19 us
    convert_element_type x1, other arithmetic, filter_per_device(): tap_low = (own - tap_high.astype(jnp.float32)).astype(jnp.bfloat16)  0.84 us
    convert_element_type x1, other arithmetic, filter_per_device(): grad_gating = (cotangent.astype(jnp.float32) * outputs).astype(jnp.bfloat16)  0.77 us
  transfers between devices with their start and end apart: 1, of which 1 were waited for; matrix products, arithmetic and copies ran while one was open for 0% of the time, Pallas kernels for 0%

profile of v1, /device:TPU:0, one launch (start us, length us, event | category | flops | bytes accessed | tf_op | source)
XLA Modules:
  0.0 34.8 jit_solution(4903830110634420038)
XLA Ops:
  0.6 0.0 copy-start.6
  0.6 0.8 %subtract_convert_fusion = (bf16[32,256]{1,0:T(8,128)(2,1)S(1)}, bf16[32,256]{1,0:T(8,128)(2,1)S(1)}) fusion(f32[32,1024]{1,0:T(8,128)} %param.12, s32[]{:T(128)S(6)} %select_n.6), kind=kLoop, calls=%fused_computation.17 | loop fusion | flops 24576 | bytes 81924 | tf_op jit(solution)/shard_map/convert_element_type | solution.py:163
  1.5 0.0 copy-done.6
  1.5 0.0 copy-start.4
  1.5 0.0 copy-start.5
  1.6 0.8 %copy-done.4 = bf16[32,1024]{1,0:T(8,128)(2,1)S(1)} copy-done((bf16[32,1024]{1,0:T(8,128)(2,1)S(1)}, bf16[32,1024]{1,0:T(8,128)(2,1)}, u32[]{:S(2)}) %copy-start.4) | copy-done | bytes 65560
  2.4 0.0 copy-done.5
  2.4 0.0 copy-start.2
  2.5 0.0 copy-start.3
  2.5 0.1 fusion.6
  2.6 0.0 copy-start
  2.6 0.0 copy-start.1
  2.6 16.0 %all_to_all.10.got_ref = bf16[32,24,128]{2,1,0:T(8,128)(2,1)S(1)} all-to-all(bf16[32,24,128]{2,1,0:T(8,128)(2,1)S(1)} %fusion.6), channel_id=1, replica_groups=mesh['ctx'=8,'chan'=4] {'ctx','chan'}, dimensions={0} | all-to-all | bytes 393216 | tf_op jit(solution)/shard_map/all_to_all | solution.py:167
  18.6 0.0 copy-done.2
  18.6 0.0 copy-done.3
  18.6 0.0 copy-done
  18.6 0.0 copy-done.1
  18.6 2.5 %spectral_products.1 = bf16[32,24,128]{2,1,0:T(8,128)(2,1)} custom-call(bf16[32,24,128]{2,1,0:T(8,128)(2,1)S(1)} %all_to_all.10.got_ref, bf16[160,256]{1,0:T(8,128)(2,1)S(1)} %copy-done.2, f32[2,80,128]{2,1,0:T(8,128)S(1)} %copy-done.1, bf16[2,256,256]{2,1,0:T(8,128)(2,1)S(1)} %copy-done, bf16[128,160]{1,0:T(8,128)(2,1)S(1)} %copy-done.3), custom_call_target="tpu_custom_call" | custom-call | tf_op jit(solution)/shard_map/spectral_products/pallas_call | solution.py:137
  21.1 2.7 %all-to-all-start.1 = ((bf16[32,24,128]{2,1,0:T(8,128)(2,1)}), bf16[32,24,128]{2,1,0:T(8,128)(2,1)S(1)}, u32[]{:S(2)}, u32[]{:S(2)}) async-start(bf16[32,24,128]{2,1,0:T(8,128)(2,1)} %spectral_products.1), calls=%async_computation.1 | async-start | bytes 393216 | tf_op jit(solution)/shard_map/all_to_all | solution.py:170
  23.8 8.9 %all-to-all-done.1 = bf16[32,24,128]{2,1,0:T(8,128)(2,1)S(1)} async-done(((bf16[32,24,128]{2,1,0:T(8,128)(2,1)}), bf16[32,24,128]{2,1,0:T(8,128)(2,1)S(1)}, u32[]{:S(2)}, u32[]{:S(2)}) %all-to-all-start.1) | async-done | bytes 196640 | tf_op jit(solution)/shard_map/all_to_all | solution.py:170
  32.7 0.6 %copy.20 = f32[1,8,8,128]{3,1,2,0:T(8,128)} copy(f32[1,8,8,128]{3,2,1,0:T(8,128)S(1)} %dynamic-slice_bitcast_fusion) | data formatting | bytes 65536
  33.4 0.0 copy-start.7
  33.4 0.7 %copy-done.7 = f32[32]{0:T(128)S(1)} copy-done((f32[32]{0:T(128)S(1)}, f32[32]{0:T(128)}, u32[]{:S(2)}) %copy-start.7) | copy-done | bytes 152
  34.0 0.8 %fusion.8 = (bf16[32,1024]{1,0:T(8,128)(2,1)}, bf16[32,1024]{1,0:T(8,128)(2,1)}) fusion(bf16[32,1024]{1,0:T(8,128)(2,1)S(1)} %copy-done.4, f32[4,8,8,128]{3,2,1,0:T(8,128)S(1)} %bitcast.20, bf16[32,1024]{1,0:T(8,128)(2,1)S(1)} %copy-done.6, f32[32]{0:T(128)S(1)} %copy-done.7, bf16[32,1024]{1,0:T(8,128)(2,1)S(1)} %copy-done.5, f32[4,8,8,128]{3,2,1,0:T(8,128)S(1)} %bitcast.21), kind=kLoop, calls=%fused_computation.11 | loop fusion | flops 425984 | bytes 589952 | tf_op jit(solution)/shard_map/convert_element_type | solution.py:175
  (7 shorter events, 0.1 us)
Async XLA Ops:
  0.6 0.9 %copy-start.6 = (bf16[32,1024]{1,0:T(8,128)(2,1)S(1)}, bf16[32,1024]{1,0:T(8,128)(2,1)}, u32[]{:S(2)}) copy-start(bf16[32,1024]{1,0:T(8,128)(2,1)} %param.9) | copy-start | bytes 196612
  1.5 0.8 %copy-start.4 = (bf16[32,1024]{1,0:T(8,128)(2,1)S(1)}, bf16[32,1024]{1,0:T(8,128)(2,1)}, u32[]{:S(2)}) copy-start(bf16[32,1024]{1,0:T(8,128)(2,1)} %param.11) | copy-start | bytes 196612
  1.5 0.9 %copy-start.5 = (bf16[32,1024]{1,0:T(8,128)(2,1)S(1)}, bf16[32,1024]{1,0:T(8,128)(2,1)}, u32[]{:S(2)}) copy-start(bf16[32,1024]{1,0:T(8,128)(2,1)} %param.10) | copy-start | bytes 196612
  2.4 16.1 %copy-start.2 = (bf16[160,256]{1,0:T(8,128)(2,1)S(1)}, bf16[160,256]{1,0:T(8,128)(2,1)}, u32[]{:S(2)}) copy-start(bf16[160,256]{1,0:T(8,128)(2,1)} %constant.24.clone.first_ref) | copy-start | bytes 245764
  2.5 16.1 %copy-start.3 = (bf16[128,160]{1,0:T(8,128)(2,1)S(1)}, bf16[128,160]{1,0:T(8,128)(2,1)}, u32[]{:S(2)}) copy-start(bf16[128,160]{1,0:T(8,128)(2,1)} %constant.27.clone.last_ref) | copy-start | bytes 122884
  2.6 16.0 %copy-start = (bf16[2,256,256]{2,1,0:T(8,128)(2,1)S(1)}, bf16[2,256,256]{2,1,0:T(8,128)(2,1)}, u32[]{:S(2)}) copy-start(bf16[2,256,256]{2,1,0:T(8,128)(2,1)} %constant.26.clone.second_ref) | copy-start | bytes 786436
  2.6 16.0 %copy-start.1 = (f32[2,80,128]{2,1,0:T(8,128)S(1)}, f32[2,80,128]{2,1,0:T(8,128)}, u32[]{:S(2)}) copy-start(f32[2,80,128]{2,1,0:T(8,128)} %constant.25.clone.twiddle_ref) | copy-start | bytes 245764
  21.1 11.6 %all-to-all-start.1 = ((bf16[32,24,128]{2,1,0:T(8,128)(2,1)}), bf16[32,24,128]{2,1,0:T(8,128)(2,1)S(1)}, u32[]{:S(2)}, u32[]{:S(2)}) async-start(bf16[32,24,128]{2,1,0:T(8,128)(2,1)} %spectral_products.1), calls=%async_computation.1 | async-start | bytes 393216 | tf_op jit(solution)/shard_map/all_to_all | solution.py:170
  33.4 0.7 %copy-start.7 = (f32[32]{0:T(128)S(1)}, f32[32]{0:T(128)}, u32[]{:S(2)}) copy-start(f32[32]{0:T(128)} %param.13) | copy-start | bytes 388

commit v2 on v1

--- a/solution.py
+++ b/solution.py
@@ -145,38 +145,103 @@
             pltpu.VMEM((total, 2 * LANES), jnp.float32),
             pltpu.VMEM((2, 2 * kept, (2 * groups + 1) * LANES), jnp.bfloat16),
         ],
-        compiler_params=pltpu.CompilerParams(vmem_limit_bytes=40 * 2**20),
+        compiler_params=pltpu.CompilerParams(vmem_limit_bytes=24 * 2**20),
         name="spectral_products",
     )(got, *[jnp.asarray(table) for table in tables])
+
+
+def tile_rows(values):
+    return values.reshape(values.shape[0], values.shape[1] // LANES, LANES)
+
+
+def pack_kernel(
+    groups, signal_hbm, gating_hbm, cotangent_hbm, filters_hbm, message_ref, signal_ref, gating_ref, cotangent_ref, taps_ref, sems
+):
+    channels, length = signal_ref.shape
+    share = length // groups
+    start = pl.multiple_of(lax.axis_index("chan") * share, share)
+    copies = [
+        pltpu.make_async_copy(source, target, sems.at[at])
+        for at, (source, target) in enumerate(
+            [
+                (cotangent_hbm, cotangent_ref),
+                (gating_hbm, gating_ref),
+                (signal_hbm, signal_ref),
+                (filters_hbm.at[:, pl.ds(start, share)], taps_ref),
+            ]
+        )
+    ]
+    for copy in copies:
+        copy.start()
+    for copy in copies:
+        copy.wait()
+    signal = signal_ref[...].astype(jnp.float32)
+    gated = cotangent_ref[...].astype(jnp.float32) * gating_ref[...].astype(jnp.float32)
+    high, low = split(taps_ref[...])
+    spare = message_ref.shape[1] * LANES - 2 * length - 2 * share
+    parts = [signal, gated, high.astype(jnp.float32), low.astype(jnp.float32)]
+    parts.append(jnp.zeros((channels, spare), jnp.float32))
+    message_ref[...] = tile_rows(jnp.concatenate(parts, axis=1)).astype(jnp.bfloat16)
+
+
+def pack(signal, gating, cotangent, filters, groups):
+    channels, length = signal.shape
+    vmem = pl.BlockSpec(memory_space=pltpu.VMEM)
+    return pl.pallas_call(
+        functools.partial(pack_kernel, groups),
+        out_shape=jax.ShapeDtypeStruct((channels, 3 * (length // LANES), LANES), jnp.bfloat16),
+        in_specs=[pl.BlockSpec(memory_space=pltpu.HBM)] * 4,
+        out_specs=vmem,
+        scratch_shapes=[pltpu.VMEM(signal.shape, jnp.bfloat16)] * 3
+        + [pltpu.VMEM((filters.shape[0], length // groups), jnp.float32), pltpu.SemaphoreType.DMA((4,))],
+        compiler_params=pltpu.CompilerParams(vmem_limit_bytes=16 * 2**20),
+        name="pack",
+    )(*[pltpu.with_memory_space_constraint(array, pltpu.HBM) for array in (signal, gating, cotangent, filters)])
+
+
+def finish_kernel(groups, home_ref, signal_ref, gating_ref, cotangent_ref, weight_ref, signal_out, gating_out, filters_out):
+    channels, length = signal_ref.shape
+    piece = length // LANES
+    share = channels // groups
+    home = home_ref[...].astype(jnp.float32).reshape(channels, 3 * length)
+    cotangent = cotangent_ref[...].astype(jnp.float32)
+    gated = (cotangent * gating_ref[...].astype(jnp.float32)).astype(jnp.bfloat16).astype(jnp.float32)
+    weight = weight_ref[...]
+    outputs = home[:, :length] + weight * signal_ref[...].astype(jnp.float32)
+    gating_out[...] = (cotangent * outputs).astype(jnp.bfloat16)
+    signal_out[...] = (home[:, length : 2 * length] + weight * gated).astype(jnp.bfloat16)
+    first = pl.multiple_of(lax.axis_index("chan") * share, share)
+    corr = home_ref[pl.ds(first, share), 2 * piece :, :].astype(jnp.float32)
+    filters_out[...] = corr.reshape(share, length)
+
+
+def finish(home, signal, gating, cotangent, skip_weight, groups):
+    channels, length = signal.shape
+    vmem = pl.BlockSpec(memory_space=pltpu.VMEM)
+    return pl.pallas_call(
+        functools.partial(finish_kernel, groups),
+        out_shape=(
+            jax.ShapeDtypeStruct(signal.shape, jnp.bfloat16),
+            jax.ShapeDtypeStruct(signal.shape, jnp.bfloat16),
+            jax.ShapeDtypeStruct((channels // groups, length), jnp.float32),
+        ),
+        in_specs=[vmem] * 5,
+        out_specs=(vmem,) * 3,
+        compiler_params=pltpu.CompilerParams(vmem_limit_bytes=16 * 2**20),
+        name="finish",
+    )(home, signal, gating, cotangent, skip_weight[:, None])
 
 
 def filter_per_device(signal, gating, cotangent, filters, skip_weight):
     peers = lax.axis_size("ctx")
     groups = lax.axis_size("chan")
-    channels, length = signal.shape
-    piece = length // LANES
-    taps = piece // groups
     both_axes = ("ctx", "chan")
-    gated_grad = (cotangent.astype(jnp.float32) * gating.astype(jnp.float32)).astype(jnp.bfloat16)
-    own = lax.dynamic_slice_in_dim(filters, lax.axis_index("chan") * (length // groups), length // groups, axis=1)
-    tap_high = own.astype(jnp.bfloat16)
-    tap_low = (own - tap_high.astype(jnp.float32)).astype(jnp.bfloat16)
-    tiles = lambda array: array.reshape(channels, -1, LANES)
-    message = jnp.concatenate([tiles(signal), tiles(gated_grad), tiles(tap_high), tiles(tap_low)], axis=1)
-    message = jnp.pad(message, ((0, 0), (0, 3 * piece - message.shape[1]), (0, 0)))
+    message = pack(signal, gating, cotangent, filters, groups)
     got = lax.all_to_all(message, both_axes, split_axis=0, concat_axis=0, tiled=True)
-    scale = 1.0 / math.sqrt(length * peers * groups)
+    scale = 1.0 / math.sqrt(signal.shape[1] * peers * groups)
     result = spectral_products(got, groups, peers, scale)
-    home = lax.all_to_all(result, both_axes, split_axis=0, concat_axis=0, tiled=True).astype(jnp.float32)
-    conv = home[:, :piece].reshape(channels, length)
-    back = home[:, piece : 2 * piece].reshape(channels, length)
-    weight = skip_weight[:, None]
-    outputs = conv + weight * signal.astype(jnp.float32)
-    grad_gating = (cotangent.astype(jnp.float32) * outputs).astype(jnp.bfloat16)
-    grad_signal = (back + weight * gated_grad.astype(jnp.float32)).astype(jnp.bfloat16)
-    share = channels // groups
-    corr = lax.dynamic_slice_in_dim(home[:, 2 * piece :], lax.axis_index("chan") * share, share, axis=0)
-    return (grad_signal, grad_gating, corr.reshape(share, length))
+    home = lax.all_to_all(result, both_axes, split_axis=0, concat_axis=0, tiled=True)
+    return finish(home, signal, gating, cotangent, skip_weight, groups)
 
 
 def product(form, left, right):

time: 35.2 us -> 33.1 us (0.940)
  Pallas kernels: 2.48 us -> 4.3 us
  other arithmetic: 1.72 us -> 0 us
  local copies, waits for them, and re-layouts: 2.24 us -> 0.78 us
  waiting for transfers between devices: 8.89 us -> 8.14 us
    pallas_call x0 -> x2, Pallas kernels: none -> 1.82 us  [the longest x1 1.06 us: pack(): pl.pallas_call(functools.partial(pack_kernel, groups), out_shape=jax.Shap...]
    convert_element_type x2 -> x0, other arithmetic: 1.62 us -> none  [the longest x1 0.84 us: filter_per_device(): tap_low = (own - tap_high.astype(jnp.float32)).astype(jnp.bfloat16)]
    unnamed x20 -> x16, local copies, waits for them, and re-layouts: 2.19 us -> 0.69 us
    all_to_all x1, waiting for transfers between devices: 8.89 us -> 8.14 us  [filter_per_device(): lax.all_to_all(result, both_axes, split_axis=0, concat_axis=0, tiled=True)]
where the time goes in v2:
time: 33.1 us; the launch traced here: 32.6 us
  blocking collectives  16 us (48%)
  waiting for transfers between devices  8.14 us (25%)
  Pallas kernels  4.3 us (13%)
  starting transfers between devices  2.72 us (8%)
  local copies, waits for them, and re-layouts  0.78 us (2%)
  between operations  0.71 us (2%)
    all_to_all x1, blocking collectives, filter_per_device(): lax.all_to_all(message, both_axes, split_axis=0, concat_axis=0, tiled=True)  16 us
    all_to_all x1, waiting for transfers between devices, filter_per_device(): lax.all_to_all(result, both_axes, split_axis=0, concat_axis=0, tiled=True)  8.14 us
    all_to_all x1, starting transfers between devices, filter_per_device(): lax.all_to_all(result, both_axes, split_axis=0, concat_axis=0, tiled=True)  2.72 us
    pallas_call x1, Pallas kernels, spectral_products(): pl.pallas_call(functools.partial(spectral_kernel, groups, peers, scale),...  2.48 us
    pallas_call x1, Pallas kernels, pack(): pl.pallas_call(functools.partial(pack_kernel, groups), out_shape=jax.Shap...  1.06 us
    pallas_call x1, Pallas kernels, finish(): pl.pallas_call(functools.partial(finish_kernel, groups), out_shape=(jax.S...  0.76 us
    unnamed x16, local copies, waits for them, and re-layouts  0.69 us
  transfers between devices with their start and end apart: 1, of which 1 were waited for; matrix products, arithmetic and copies ran while one was open for 0% of the time, Pallas kernels for 0%

profile of v2, /device:TPU:0, one launch (start us, length us, event | category | flops | bytes accessed | tf_op | source)
XLA Modules:
  0.0 32.6 jit_solution(927476752580720767)
XLA Ops:
  0.6 0.0 copy-start.5
  0.6 0.0 copy-start.6
  0.7 1.1 %pack.1 = bf16[32,24,128]{2,1,0:T(8,128)(2,1)S(1)} custom-call(bf16[32,1024]{1,0:T(8,128)(2,1)} %signal_ref.1, bf16[32,1024]{1,0:T(8,128)(2,1)} %gating_ref.1, bf16[32,1024]{1,0:T(8,128)(2,1)} %cotangent_ref.1, f32[32,1024]{1,0:T(8,128)} %filters_hbm.1), custom_call_target="tpu_custom_call" | custom-call | tf_op jit(solution)/shard_map/pack/pallas_call | solution.py:190
  1.7 0.0 copy-start
  1.7 0.0 copy-start.4
  1.8 16.0 %all_to_all.10.got_ref = bf16[32,24,128]{2,1,0:T(8,128)(2,1)S(1)} all-to-all(bf16[32,24,128]{2,1,0:T(8,128)(2,1)S(1)} %pack.1), channel_id=1, replica_groups=mesh['ctx'=8,'chan'=4] {'ctx','chan'}, dimensions={0} | all-to-all | bytes 393216 | tf_op jit(solution)/shard_map/all_to_all | solution.py:240
  17.7 0.0 copy-done.5
  17.7 0.0 copy-done.6
  17.7 0.0 copy-done
  17.8 0.0 copy-done.4
  17.8 2.5 %spectral_products.1 = bf16[32,24,128]{2,1,0:T(8,128)(2,1)} custom-call(bf16[32,24,128]{2,1,0:T(8,128)(2,1)S(1)} %all_to_all.10.got_ref, bf16[160,256]{1,0:T(8,128)(2,1)S(1)} %copy-done.4, f32[2,80,128]{2,1,0:T(8,128)S(1)} %copy-done.5, bf16[2,256,256]{2,1,0:T(8,128)(2,1)S(1)} %copy-done, bf16[128,160]{1,0:T(8,128)(2,1)S(1)} %copy-done.6), custom_call_target="tpu_custom_call" | custom-call | tf_op jit(solution)/shard_map/spectral_products/pallas_call | solution.py:137
  20.2 0.0 copy-start.1
  20.2 0.0 copy-start.2
  20.2 0.0 copy-start.3
  20.3 2.7 %all-to-all-start.1 = ((bf16[32,24,128]{2,1,0:T(8,128)(2,1)}), bf16[32,24,128]{2,1,0:T(8,128)(2,1)S(1)}, u32[]{:S(2)}, u32[]{:S(2)}) async-start(bf16[32,24,128]{2,1,0:T(8,128)(2,1)} %spectral_products.1), calls=%async_computation.1 | async-start | bytes 393216 | tf_op jit(solution)/shard_map/all_to_all | solution.py:243
  23.0 0.0 copy-start.7
  23.0 0.6 %copy-done.7 = f32[32]{0:T(128)S(1)} copy-done((f32[32]{0:T(128)S(1)}, f32[32]{0:T(128)}, u32[]{:S(2)}) %copy-start.7) | copy-done | bytes 152
  23.6 0.1 copy.12.weight_ref
  23.7 8.1 %all-to-all-done.1.home_ref = bf16[32,24,128]{2,1,0:T(8,128)(2,1)S(1)} async-done(((bf16[32,24,128]{2,1,0:T(8,128)(2,1)}), bf16[32,24,128]{2,1,0:T(8,128)(2,1)S(1)}, u32[]{:S(2)}, u32[]{:S(2)}) %all-to-all-start.1) | async-done | bytes 196640 | tf_op jit(solution)/shard_map/all_to_all | solution.py:243
  31.9 0.0 copy-done.1
  31.9 0.0 copy-done.2
  31.9 0.0 copy-done.3
  31.9 0.8 %finish.1 = (bf16[32,1024]{1,0:T(8,128)(2,1)}, bf16[32,1024]{1,0:T(8,128)(2,1)}, f32[8,1024]{1,0:T(8,128)}) custom-call(bf16[32,24,128]{2,1,0:T(8,128)(2,1)S(1)} %all-to-all-done.1.home_ref, bf16[32,1024]{1,0:T(8,128)(2,1)S(1)} %copy-done.1, bf16[32,1024]{1,0:T(8,128)(2,1)S(1)} %copy-done.2, bf16[32,1024]{1,0:T(8,128)(2,1)S(1)} %copy-done.3, ...), custom_call_target="tpu_custom_call" | custom-call | tf_op jit(solution)/shard_map/finish/pallas_call | solution.py:221
Async XLA Ops:
  0.6 17.1 %copy-start.5 = (f32[2,80,128]{2,1,0:T(8,128)S(1)}, f32[2,80,128]{2,1,0:T(8,128)}, u32[]{:S(2)}) copy-start(f32[2,80,128]{2,1,0:T(8,128)} %constant.9.clone.twiddle_ref) | copy-start | bytes 245764
  0.6 17.1 %copy-start.6 = (bf16[128,160]{1,0:T(8,128)(2,1)S(1)}, bf16[128,160]{1,0:T(8,128)(2,1)}, u32[]{:S(2)}) copy-start(bf16[128,160]{1,0:T(8,128)(2,1)} %constant.11.clone.last_ref) | copy-start | bytes 122884
  1.7 16.0 %copy-start = (bf16[2,256,256]{2,1,0:T(8,128)(2,1)S(1)}, bf16[2,256,256]{2,1,0:T(8,128)(2,1)}, u32[]{:S(2)}) copy-start(bf16[2,256,256]{2,1,0:T(8,128)(2,1)} %constant.10.clone.second_ref) | copy-start | bytes 786436
  1.7 16.0 %copy-start.4 = (bf16[160,256]{1,0:T(8,128)(2,1)S(1)}, bf16[160,256]{1,0:T(8,128)(2,1)}, u32[]{:S(2)}) copy-start(bf16[160,256]{1,0:T(8,128)(2,1)} %constant.8.clone.first_ref) | copy-start | bytes 245764
  20.2 11.6 %copy-start.1 = (bf16[32,1024]{1,0:T(8,128)(2,1)S(1)}, bf16[32,1024]{1,0:T(8,128)(2,1)}, u32[]{:S(2)}) copy-start(bf16[32,1024]{1,0:T(8,128)(2,1)} %signal_ref.1) | copy-start | bytes 196612
  20.2 11.6 %copy-start.2 = (bf16[32,1024]{1,0:T(8,128)(2,1)S(1)}, bf16[32,1024]{1,0:T(8,128)(2,1)}, u32[]{:S(2)}) copy-start(bf16[32,1024]{1,0:T(8,128)(2,1)} %gating_ref.1) | copy-start | bytes 196612
  20.2 11.6 %copy-start.3 = (bf16[32,1024]{1,0:T(8,128)(2,1)S(1)}, bf16[32,1024]{1,0:T(8,128)(2,1)}, u32[]{:S(2)}) copy-start(bf16[32,1024]{1,0:T(8,128)(2,1)} %cotangent_ref.1) | copy-start | bytes 196612
  20.3 11.6 %all-to-all-start.1 = ((bf16[32,24,128]{2,1,0:T(8,128)(2,1)}), bf16[32,24,128]{2,1,0:T(8,128)(2,1)S(1)}, u32[]{:S(2)}, u32[]{:S(2)}) async-start(bf16[32,24,128]{2,1,0:T(8,128)(2,1)} %spectral_products.1), calls=%async_computation.1 | async-start | bytes 393216 | tf_op jit(solution)/shard_map/all_to_all | solution.py:243
  23.0 0.7 %copy-start.7 = (f32[32]{0:T(128)S(1)}, f32[32]{0:T(128)}, u32[]{:S(2)}) copy-start(f32[32]{0:T(128)} %param.13) | copy-start | bytes 388

commit v3 on v2

--- a/solution.py
+++ b/solution.py
@@ -21,26 +21,19 @@
 def dft_tables(rows):
     height = 2 * rows
     padded = height * LANES
-    kept = rows + 1
-    pad = -kept % 16
-    k1 = np.arange(kept)
+    k1 = np.arange(rows)
     n1 = np.arange(rows)
     n2 = np.arange(LANES)
-    zeros = lambda table, axis: np.pad(table, [(0, pad if a == axis else 0) for a in range(2)])
-    outer = 2.0 * np.pi * (np.outer(k1, n1) % height) / height
-    first = np.concatenate([zeros(np.cos(outer), 0), zeros(-np.sin(outer), 0)], axis=0)
-    high, low = split_table(first)
+    outer = np.pi * (np.outer(2 * k1 + 1, n1) % (2 * height)) / height
+    high, low = split_table(np.concatenate([np.cos(outer), -np.sin(outer)], axis=0))
     first = np.concatenate([high, low, high, low], axis=1)
-    turn = 2.0 * np.pi * (np.outer(k1, n2) % padded) / padded
-    twiddle = np.stack([zeros(np.cos(turn), 0), zeros(np.sin(turn), 0)]).astype(np.float32)
+    turn = np.pi * (np.outer(2 * k1 + 1, n2) % (2 * padded)) / padded
+    twiddle = np.stack([np.cos(turn), np.sin(turn)]).astype(np.float32)
     inner = 2.0 * np.pi * (np.outer(n2, n2) % LANES) / LANES
     cosine, sine = np.cos(inner), np.sin(inner)
     second = np.stack(split_table(np.block([[cosine, -sine], [sine, cosine]])))
-    weight = np.where((k1 == 0) | (k1 == rows), 1.0, 2.0) / padded
-    last = np.concatenate(
-        [zeros(np.cos(outer.T) * weight, 1), zeros(-np.sin(outer.T) * weight, 1)], axis=1
-    )
-    last = np.concatenate(split_table(last), axis=0)
+    high, low = split_table(np.concatenate([np.cos(outer.T), -np.sin(outer.T)], axis=1) * (2.0 / padded))
+    last = np.block([[high, high], [low, np.zeros_like(low)]])
     return first, twiddle, second, last
 
 
@@ -116,10 +109,10 @@
         imag, real = both[:, :LANES], both[:, LANES:]
         turned = jnp.concatenate([real * cosine - imag * sine, imag * cosine + real * sine], axis=0)
         high, low = split(turned)
-        back_ref[0, :, sequence * LANES : (sequence + 1) * LANES] = high
-        back_ref[1, :, sequence * LANES : (sequence + 1) * LANES] = low
-    both = dot(last_ref[...], back_ref[0])
-    result = both[:rows] + both[rows:] + dot(last_ref[:rows], back_ref[1])
+        back_ref[: 2 * kept, sequence * LANES : (sequence + 1) * LANES] = high
+        back_ref[2 * kept :, sequence * LANES : (sequence + 1) * LANES] = low
+    both = dot(last_ref[...], back_ref[...])
+    result = both[:rows] + both[rows:]
     for peer in range(peers):
         piece_rows = result[peer * piece : (peer + 1) * piece]
         for group in range(groups):
@@ -143,7 +136,7 @@
             pltpu.VMEM((2 * rows, 2 * groups * LANES), jnp.bfloat16),
             pltpu.VMEM((2 * total, 2 * LANES), jnp.bfloat16),
             pltpu.VMEM((total, 2 * LANES), jnp.float32),
-            pltpu.VMEM((2, 2 * kept, (2 * groups + 1) * LANES), jnp.bfloat16),
+            pltpu.VMEM((4 * kept, (2 * groups + 1) * LANES), jnp.bfloat16),
         ],
         compiler_params=pltpu.CompilerParams(vmem_limit_bytes=24 * 2**20),
         name="spectral_products",
@@ -155,7 +148,20 @@
 
 
 def pack_kernel(
-    groups, signal_hbm, gating_hbm, cotangent_hbm, filters_hbm, message_ref, signal_ref, gating_ref, cotangent_ref, taps_ref, sems
+    groups,
+    signal_hbm,
+    gating_hbm,
+    cotangent_hbm,
+    filters_hbm,
+    weight_hbm,
+    message_ref,
+    column_ref,
+    signal_ref,
+    gating_ref,
+    cotangent_ref,
+    taps_ref,
+    weight_ref,
+    sems,
 ):
     channels, length = signal_ref.shape
     share = length // groups
@@ -168,6 +174,7 @@
                 (gating_hbm, gating_ref),
                 (signal_hbm, signal_ref),
                 (filters_hbm.at[:, pl.ds(start, share)], taps_ref),
+                (weight_hbm, weight_ref),
             ]
         )
     ]
@@ -182,31 +189,43 @@
     parts = [signal, gated, high.astype(jnp.float32), low.astype(jnp.float32)]
     parts.append(jnp.zeros((channels, spare), jnp.float32))
     message_ref[...] = tile_rows(jnp.concatenate(parts, axis=1)).astype(jnp.bfloat16)
-
-
-def pack(signal, gating, cotangent, filters, groups):
+    square = (channels, channels)
+    diagonal = lax.broadcasted_iota(jnp.int32, square, 0) == lax.broadcasted_iota(jnp.int32, square, 1)
+    weight = jnp.sum(jnp.where(diagonal, jnp.broadcast_to(weight_ref[...], square), 0.0), axis=1, keepdims=True)
+    column_ref[...] = jnp.broadcast_to(weight, column_ref.shape)
+
+
+def pack(signal, gating, cotangent, filters, skip_weight, groups):
     channels, length = signal.shape
     vmem = pl.BlockSpec(memory_space=pltpu.VMEM)
+    operands = (signal, gating, cotangent, filters, skip_weight[None, :])
     return pl.pallas_call(
         functools.partial(pack_kernel, groups),
-        out_shape=jax.ShapeDtypeStruct((channels, 3 * (length // LANES), LANES), jnp.bfloat16),
-        in_specs=[pl.BlockSpec(memory_space=pltpu.HBM)] * 4,
-        out_specs=vmem,
+        out_shape=(
+            jax.ShapeDtypeStruct((channels, 3 * (length // LANES), LANES), jnp.bfloat16),
+            jax.ShapeDtypeStruct((channels, LANES), jnp.float32),
+        ),
+        in_specs=[pl.BlockSpec(memory_space=pltpu.HBM)] * 5,
+        out_specs=(vmem, vmem),
         scratch_shapes=[pltpu.VMEM(signal.shape, jnp.bfloat16)] * 3
-        + [pltpu.VMEM((filters.shape[0], length // groups), jnp.float32), pltpu.SemaphoreType.DMA((4,))],
+        + [
+            pltpu.VMEM((filters.shape[0], length // groups), jnp.float32),
+            pltpu.VMEM((1, channels), jnp.float32),
+            pltpu.SemaphoreType.DMA((5,)),
+        ],
         compiler_params=pltpu.CompilerParams(vmem_limit_bytes=16 * 2**20),
         name="pack",
-    )(*[pltpu.with_memory_space_constraint(array, pltpu.HBM) for array in (signal, gating, cotangent, filters)])
-
-
-def finish_kernel(groups, home_ref, signal_ref, gating_ref, cotangent_ref, weight_ref, signal_out, gating_out, filters_out):
+    )(*[pltpu.with_memory_space_constraint(operand, pltpu.HBM) for operand in operands])
+
+
+def finish_kernel(groups, home_ref, signal_ref, gating_ref, cotangent_ref, column_ref, signal_out, gating_out, filters_out):
     channels, length = signal_ref.shape
     piece = length // LANES
     share = channels // groups
     home = home_ref[...].astype(jnp.float32).reshape(channels, 3 * length)
     cotangent = cotangent_ref[...].astype(jnp.float32)
     gated = (cotangent * gating_ref[...].astype(jnp.float32)).astype(jnp.bfloat16).astype(jnp.float32)
-    weight = weight_ref[...]
+    weight = column_ref[:, :1]
     outputs = home[:, :length] + weight * signal_ref[...].astype(jnp.float32)
     gating_out[...] = (cotangent * outputs).astype(jnp.bfloat16)
     signal_out[...] = (home[:, length : 2 * length] + weight * gated).astype(jnp.bfloat16)
@@ -215,7 +234,7 @@
     filters_out[...] = corr.reshape(share, length)
 
 
-def finish(home, signal, gating, cotangent, skip_weight, groups):
+def finish(home, signal, gating, cotangent, column, groups):
     channels, length = signal.shape
     vmem = pl.BlockSpec(memory_space=pltpu.VMEM)
     return pl.pallas_call(
@@ -229,19 +248,19 @@
         out_specs=(vmem,) * 3,
         compiler_params=pltpu.CompilerParams(vmem_limit_bytes=16 * 2**20),
         name="finish",
-    )(home, signal, gating, cotangent, skip_weight[:, None])
+    )(home, signal, gating, cotangent, column)
 
 
 def filter_per_device(signal, gating, cotangent, filters, skip_weight):
     peers = lax.axis_size("ctx")
     groups = lax.axis_size("chan")
     both_axes = ("ctx", "chan")
-    message = pack(signal, gating, cotangent, filters, groups)
+    message, column = pack(signal, gating, cotangent, filters, skip_weight, groups)
     got = lax.all_to_all(message, both_axes, split_axis=0, concat_axis=0, tiled=True)
     scale = 1.0 / math.sqrt(signal.shape[1] * peers * groups)
     result = spectral_products(got, groups, peers, scale)
     home = lax.all_to_all(result, both_axes, split_axis=0, concat_axis=0, tiled=True)
-    return finish(home, signal, gating, cotangent, skip_weight, groups)
+    return finish(home, signal, gating, cotangent, column, groups)
 
 
 def product(form, left, right):

time: 33.1 us -> 31.9 us (0.964)
  blocking collectives: 16 us -> 27.4 us
  waiting for transfers between devices: 8.14 us -> 0 us
  starting transfers between devices: 2.72 us -> 0 us
  Pallas kernels: 4.3 us -> 3.38 us
  local copies, waits for them, and re-layouts: 0.78 us -> 0.05 us
    all_to_all x0 -> x1, blocking collectives: none -> 11.4 us  [filter_per_device(): lax.all_to_all(result, both_axes, split_axis=0, concat_axis=0, tiled=True)]
    all_to_all x1 -> x0, waiting for transfers between devices: 8.14 us -> none  [filter_per_device(): lax.all_to_all(result, both_axes, split_axis=0, concat_axis=0, tiled=True)]
    all_to_all x1 -> x0, starting transfers between devices: 2.72 us -> none  [filter_per_device(): lax.all_to_all(result, both_axes, split_axis=0, concat_axis=0, tiled=True)]
    pallas_call x1, Pallas kernels: 2.48 us -> 1.53 us  [spectral_products(): pl.pallas_call(functools.partial(spectral_kernel, groups, peers, scale),...]
    unnamed x16 -> x14, local copies, waits for them, and re-layouts: 0.69 us -> 0.05 us
  transfers between devices with their start and end apart: 1 -> 0, of which waited for: 1 -> 0; matrix products, arithmetic and copies ran while one was open for 0% -> 0% of each run, Pallas kernels for 0% -> 0%
where the time goes in v3:
time: 31.9 us; the launch traced here: 31.5 us
  blocking collectives  27.4 us (86%)
  Pallas kernels  3.38 us (11%)
  between operations  0.72 us (2%)
    all_to_all x1, blocking collectives, filter_per_device(): lax.all_to_all(message, both_axes, split_axis=0, concat_axis=0, tiled=True)  16 us
    all_to_all x1, blocking collectives, filter_per_device(): lax.all_to_all(result, both_axes, split_axis=0, concat_axis=0, tiled=True)  11.4 us
    pallas_call x1, Pallas kernels, spectral_products(): pl.pallas_call(functools.partial(spectral_kernel, groups, peers, scale),...  1.53 us
    pallas_call x1, Pallas kernels, pack(): pl.pallas_call(functools.partial(pack_kernel, groups), out_shape=(jax.Sha...  1.09 us
    pallas_call x1, Pallas kernels, finish(): pl.pallas_call(functools.partial(finish_kernel, groups), out_shape=(jax.S...  0.76 us

profile of v3, /device:TPU:0, one launch (start us, length us, event | category | flops | bytes accessed | tf_op | source)
XLA Modules:
  0.0 31.5 jit_solution(15406218143396449750)
XLA Ops:
  0.6 0.0 copy-start.6
  0.6 1.1 %pack.1 = (bf16[32,24,128]{2,1,0:T(8,128)(2,1)S(1)}, f32[32,128]{1,0:T(8,128)S(1)}) custom-call(bf16[32,1024]{1,0:T(8,128)(2,1)} %signal_ref.1, bf16[32,1024]{1,0:T(8,128)(2,1)} %gating_ref.1, bf16[32,1024]{1,0:T(8,128)(2,1)} %cotangent_ref.1, f32[32,1024]{1,0:T(8,128)} %filters_hbm.1, f32[1,32]{1,0:T(1,128)} %bitcast.1), custom_call_target="tpu_custom_call" | custom-call | tf_op jit(solution)/shard_map/pack/pallas_call | solution.py:202
  1.7 0.0 copy-start.3
  1.7 0.0 copy-start.4
  1.8 0.0 copy-start.5
  1.8 16.0 %all_to_all.10.got_ref = bf16[32,24,128]{2,1,0:T(8,128)(2,1)S(1)} all-to-all(bf16[32,24,128]{2,1,0:T(8,128)(2,1)S(1)} %get-tuple-element.5), channel_id=1, replica_groups=mesh['ctx'=8,'chan'=4] {'ctx','chan'}, dimensions={0} | all-to-all | bytes 393216 | tf_op jit(solution)/shard_map/all_to_all | solution.py:259
  17.8 0.0 copy-done.6
  17.8 0.0 copy-done.3
  17.8 0.0 copy-done.4
  17.8 0.0 copy-done.5
  17.8 1.5 %spectral_products.1 = bf16[32,24,128]{2,1,0:T(8,128)(2,1)S(1)} custom-call(bf16[32,24,128]{2,1,0:T(8,128)(2,1)S(1)} %all_to_all.10.got_ref, bf16[128,256]{1,0:T(8,128)(2,1)S(1)} %copy-done.6, f32[2,64,128]{2,1,0:T(8,128)S(1)} %copy-done.5, bf16[2,256,256]{2,1,0:T(8,128)(2,1)S(1)} %copy-done.3, bf16[128,256]{1,0:T(8,128)(2,1)S(1)} %copy-done.4), custom_call_target="tpu_custom_call" | custom-call | tf_op jit(solution)/shard_map/spectral_products/pallas_call | solution.py:130
  19.3 0.0 copy-start
  19.3 0.0 copy-start.1
  19.4 0.0 copy-start.2
  19.4 11.4 %all_to_all.11.home_ref = bf16[32,24,128]{2,1,0:T(8,128)(2,1)S(1)} all-to-all(bf16[32,24,128]{2,1,0:T(8,128)(2,1)S(1)} %spectral_products.1), channel_id=1, replica_groups=mesh['ctx'=8,'chan'=4] {'ctx','chan'}, dimensions={0} | all-to-all | bytes 393216 | tf_op jit(solution)/shard_map/all_to_all | solution.py:262
  30.8 0.0 copy-done
  30.8 0.0 copy-done.1
  30.8 0.0 copy-done.2
  30.8 0.8 %finish.1 = (bf16[32,1024]{1,0:T(8,128)(2,1)}, bf16[32,1024]{1,0:T(8,128)(2,1)}, f32[8,1024]{1,0:T(8,128)}) custom-call(bf16[32,24,128]{2,1,0:T(8,128)(2,1)S(1)} %all_to_all.11.home_ref, bf16[32,1024]{1,0:T(8,128)(2,1)S(1)} %copy-done, bf16[32,1024]{1,0:T(8,128)(2,1)S(1)} %copy-done.1, bf16[32,1024]{1,0:T(8,128)(2,1)S(1)} %copy-done.2, ...), custom_call_target="tpu_custom_call" | custom-call | tf_op jit(solution)/shard_map/finish/pallas_call | solution.py:240
Async XLA Ops:
  0.6 17.1 %copy-start.6 = (bf16[128,256]{1,0:T(8,128)(2,1)S(1)}, bf16[128,256]{1,0:T(8,128)(2,1)}, u32[]{:S(2)}) copy-start(bf16[128,256]{1,0:T(8,128)(2,1)} %constant.8.clone.first_ref) | copy-start | bytes 196612
  1.7 16.0 %copy-start.3 = (bf16[2,256,256]{2,1,0:T(8,128)(2,1)S(1)}, bf16[2,256,256]{2,1,0:T(8,128)(2,1)}, u32[]{:S(2)}) copy-start(bf16[2,256,256]{2,1,0:T(8,128)(2,1)} %constant.10.clone.second_ref) | copy-start | bytes 786436
  1.7 16.0 %copy-start.4 = (bf16[128,256]{1,0:T(8,128)(2,1)S(1)}, bf16[128,256]{1,0:T(8,128)(2,1)}, u32[]{:S(2)}) copy-start(bf16[128,256]{1,0:T(8,128)(2,1)} %constant.11.clone.last_ref) | copy-start | bytes 196612
  1.8 16.0 %copy-start.5 = (f32[2,64,128]{2,1,0:T(8,128)S(1)}, f32[2,64,128]{2,1,0:T(8,128)}, u32[]{:S(2)}) copy-start(f32[2,64,128]{2,1,0:T(8,128)} %constant.9.clone.twiddle_ref) | copy-start | bytes 196612
  19.3 11.4 %copy-start = (bf16[32,1024]{1,0:T(8,128)(2,1)S(1)}, bf16[32,1024]{1,0:T(8,128)(2,1)}, u32[]{:S(2)}) copy-start(bf16[32,1024]{1,0:T(8,128)(2,1)} %signal_ref.1) | copy-start | bytes 196612
  19.3 11.4 %copy-start.1 = (bf16[32,1024]{1,0:T(8,128)(2,1)S(1)}, bf16[32,1024]{1,0:T(8,128)(2,1)}, u32[]{:S(2)}) copy-start(bf16[32,1024]{1,0:T(8,128)(2,1)} %gating_ref.1) | copy-start | bytes 196612
  19.4 11.4 %copy-start.2 = (bf16[32,1024]{1,0:T(8,128)(2,1)S(1)}, bf16[32,1024]{1,0:T(8,128)(2,1)}, u32[]{:S(2)}) copy-start(bf16[32,1024]{1,0:T(8,128)(2,1)} %cotangent_ref.1) | copy-start | bytes 196612

commit v4 on v3

--- a/solution.py
+++ b/solution.py
@@ -10,6 +10,7 @@
 from jax.sharding import PartitionSpec as P
 
 LANES = 128
+TILE = 2
 
 
 def split_table(table):
@@ -31,7 +32,8 @@
     twiddle = np.stack([np.cos(turn), np.sin(turn)]).astype(np.float32)
     inner = 2.0 * np.pi * (np.outer(n2, n2) % LANES) / LANES
     cosine, sine = np.cos(inner), np.sin(inner)
-    second = np.stack(split_table(np.block([[cosine, -sine], [sine, cosine]])))
+    high, low = split_table(np.block([[cosine, -sine], [sine, cosine]]))
+    second = np.concatenate([high, high, low], axis=0)
     high, low = split_table(np.concatenate([np.cos(outer.T), -np.sin(outer.T)], axis=1) * (2.0 / padded))
     last = np.block([[high, high], [low, np.zeros_like(low)]])
     return first, twiddle, second, last
@@ -49,12 +51,12 @@
 def spectral_kernel(
     groups, peers, scale, got_ref, first_ref, twiddle_ref, second_ref, last_ref, out_ref, in_ref, part_ref, spec_ref, back_ref
 ):
-    piece = got_ref.shape[1] // 3
+    piece = out_ref.shape[1] // 3
     taps = piece // groups
     rows = peers * piece
     kept = twiddle_ref.shape[1]
     count = 2 * groups
-    got = [got_ref[source].astype(jnp.float32) for source in range(peers * groups)]
+    got = got_ref[...].astype(jnp.float32).reshape(peers * groups, -1, LANES)
 
     def gather(group, start):
         parts = [got[peer * groups + group][start : start + piece] for peer in range(peers)]
@@ -66,23 +68,30 @@
         in_ref[0:rows, sequence * LANES : (sequence + 1) * LANES] = values
         in_ref[rows : 2 * rows, sequence * LANES : (sequence + 1) * LANES] = values
     tap_high = jnp.concatenate([part[2 * piece : 2 * piece + taps] for part in got], axis=0).astype(jnp.bfloat16)
-    tap_low = jnp.concatenate([part[2 * piece + taps : 2 * piece + 2 * taps] for part in got], axis=0).astype(jnp.bfloat16)
-    tap_in = jnp.concatenate([tap_high, tap_high, tap_low, tap_low], axis=0)
+    tap_in = jnp.concatenate([tap_high, tap_high], axis=0)
     cosine, sine = twiddle_ref[0], twiddle_ref[1]
     stage = dot(first_ref[:, : 2 * rows], in_ref[...])
-    tap_stage = dot(first_ref[...], tap_in)
+    tap_stage = dot(first_ref[:, : 2 * rows], tap_in)
     total = (count + 1) * kept
+
+    def store_parts(sequence, values):
+        high, low = split(values)
+        at = slice(sequence * kept, (sequence + 1) * kept)
+        part_ref[at, : 2 * LANES] = high
+        part_ref[at, 2 * LANES : 4 * LANES] = low
+        part_ref[at, 4 * LANES :] = high
+
     for sequence in range(count + 1):
         source = tap_stage if sequence == count else stage[:, sequence * LANES : (sequence + 1) * LANES]
         real, imag = source[:kept], source[kept:]
         turned = jnp.concatenate([real * cosine + imag * sine, imag * cosine - real * sine], axis=1)
-        high, low = split(turned)
-        part_ref[sequence * kept : (sequence + 1) * kept] = high
-        part_ref[total + sequence * kept : total + (sequence + 1) * kept] = low
+        store_parts(sequence, turned)
 
     def second_stage():
-        both = dot(part_ref[...], second_ref[0])
-        spec_ref[...] = both[:total] + both[total:] + dot(part_ref[:total], second_ref[1])
+        step = pl.cdiv(total, 4 * 16) * 16
+        for at in range(0, total, step):
+            stop = min(at + step, total)
+            spec_ref[at:stop] = dot(part_ref[at:stop], second_ref[...])
 
     second_stage()
     tap = spec_ref[count * kept : total]
@@ -90,9 +99,7 @@
     corr_real = corr_imag = None
 
     def put(sequence, real, imag):
-        high, low = split(jnp.concatenate([imag, real], axis=1))
-        part_ref[sequence * kept : (sequence + 1) * kept] = high
-        part_ref[total + sequence * kept : total + (sequence + 1) * kept] = low
+        store_parts(sequence, jnp.concatenate([imag, real], axis=1))
 
     for group in range(groups):
         sig = spec_ref[group * kept : (group + 1) * kept]
@@ -121,20 +128,20 @@
             out_ref[peer * groups + group] = message.astype(jnp.bfloat16)
 
 
-def spectral_products(got, groups, peers, scale):
-    rows = peers * (got.shape[1] // 3)
+def spectral_products(got, piece, groups, peers, scale):
+    rows = peers * piece
     tables = dft_tables(rows)
     kept = tables[1].shape[1]
     total = (2 * groups + 1) * kept
     vmem = pl.BlockSpec(memory_space=pltpu.VMEM)
     return pl.pallas_call(
         functools.partial(spectral_kernel, groups, peers, scale),
-        out_shape=jax.ShapeDtypeStruct(got.shape, jnp.bfloat16),
+        out_shape=jax.ShapeDtypeStruct((got.shape[0], 3 * piece, LANES), jnp.bfloat16),
         in_specs=[vmem] * 5,
         out_specs=vmem,
         scratch_shapes=[
             pltpu.VMEM((2 * rows, 2 * groups * LANES), jnp.bfloat16),
-            pltpu.VMEM((2 * total, 2 * LANES), jnp.bfloat16),
+            pltpu.VMEM((total, 6 * LANES), jnp.bfloat16),
             pltpu.VMEM((total, 2 * LANES), jnp.float32),
             pltpu.VMEM((4 * kept, (2 * groups + 1) * LANES), jnp.bfloat16),
         ],
@@ -184,11 +191,8 @@
         copy.wait()
     signal = signal_ref[...].astype(jnp.float32)
     gated = cotangent_ref[...].astype(jnp.float32) * gating_ref[...].astype(jnp.float32)
-    high, low = split(taps_ref[...])
-    spare = message_ref.shape[1] * LANES - 2 * length - 2 * share
-    parts = [signal, gated, high.astype(jnp.float32), low.astype(jnp.float32)]
-    parts.append(jnp.zeros((channels, spare), jnp.float32))
-    message_ref[...] = tile_rows(jnp.concatenate(parts, axis=1)).astype(jnp.bfloat16)
+    rows = tile_rows(jnp.concatenate([signal, gated, taps_ref[...]], axis=1))
+    message_ref[...] = rows.reshape(message_ref.shape).astype(jnp.bfloat16)
     square = (channels, channels)
     diagonal = lax.broadcasted_iota(jnp.int32, square, 0) == lax.broadcasted_iota(jnp.int32, square, 1)
     weight = jnp.sum(jnp.where(diagonal, jnp.broadcast_to(weight_ref[...], square), 0.0), axis=1, keepdims=True)
@@ -202,7 +206,7 @@
     return pl.pallas_call(
         functools.partial(pack_kernel, groups),
         out_shape=(
-            jax.ShapeDtypeStruct((channels, 3 * (length // LANES), LANES), jnp.bfloat16),
+            jax.ShapeDtypeStruct((channels, (2 * length + length // groups) // (TILE * LANES), TILE, LANES), jnp.bfloat16),
             jax.ShapeDtypeStruct((channels, LANES), jnp.float32),
         ),
         in_specs=[pl.BlockSpec(memory_space=pltpu.HBM)] * 5,
@@ -258,7 +262,7 @@
     message, column = pack(signal, gating, cotangent, filters, skip_weight, groups)
     got = lax.all_to_all(message, both_axes, split_axis=0, concat_axis=0, tiled=True)
     scale = 1.0 / math.sqrt(signal.shape[1] * peers * groups)
-    result = spectral_products(got, groups, peers, scale)
+    result = spectral_products(got, signal.shape[1] // LANES, groups, peers, scale)
     home = lax.all_to_all(result, both_axes, split_axis=0, concat_axis=0, tiled=True)
     return finish(home, signal, gating, cotangent, column, groups)
 
@@ -492,8 +496,9 @@
     peers, groups = lax.axis_size("ctx"), lax.axis_size("chan")
     channels, length = signal.shape
     one_each = channels == filters.shape[0] == peers * groups
-    whole_tiles = length % (8 * LANES) == 0 and (length // LANES) % groups == 0
-    if one_each and whole_tiles and 2 * (length // LANES // groups) <= length // LANES:
+    piece = length // LANES
+    whole_tiles = length % (8 * LANES) == 0 and piece % groups == 0
+    if one_each and whole_tiles and (peers * piece) % 16 == 0 and (piece // groups) % TILE == 0:
         return filter_per_device(signal, gating, cotangent, filters, skip_weight)
     return split_transforms(signal, gating, cotangent, filters, skip_weight)
 

time: 31.9 us -> 30.7 us (0.962)
  blocking collectives: 27.4 us -> 26.3 us
    all_to_all x1, blocking collectives: 11.4 us -> 10.8 us  [filter_per_device(): lax.all_to_all(result, both_axes, split_axis=0, concat_axis=0, tiled=True)]
    all_to_all x1, blocking collectives: 16 us -> 15.5 us  [filter_per_device(): lax.all_to_all(message, both_axes, split_axis=0, concat_axis=0, tiled=True)]
where the time goes in v4:
time: 30.7 us; the launch traced here: 30.3 us
  blocking collectives  26.3 us (86%)
  Pallas kernels  3.21 us (10%)
  between operations  0.72 us (2%)
    all_to_all x1, blocking collectives, filter_per_device(): lax.all_to_all(message, both_axes, split_axis=0, concat_axis=0, tiled=True)  15.5 us
    all_to_all x1, blocking collectives, filter_per_device(): lax.all_to_all(result, both_axes, split_axis=0, concat_axis=0, tiled=True)  10.8 us
    pallas_call x1, Pallas kernels, spectral_products(): pl.pallas_call(functools.partial(spectral_kernel, groups, peers, scale),...  1.25 us
    pallas_call x1, Pallas kernels, pack(): pl.pallas_call(functools.partial(pack_kernel, groups), out_shape=(jax.Sha...  1.2 us
    pallas_call x1, Pallas kernels, finish(): pl.pallas_call(functools.partial(finish_kernel, groups), out_shape=(jax.S...  0.76 us

profile of v4, /device:TPU:0, one launch (start us, length us, event | category | flops | bytes accessed | tf_op | source)
XLA Modules:
  0.0 30.3 jit_solution(4687215287487323747)
XLA Ops:
  0.6 0.0 copy-start
  0.6 1.2 %pack.1 = (bf16[32,9,2,128]{3,2,1,0:T(2,128)(2,1)S(1)}, f32[32,128]{1,0:T(8,128)S(1)}) custom-call(bf16[32,1024]{1,0:T(8,128)(2,1)} %signal_ref.1, bf16[32,1024]{1,0:T(8,128)(2,1)} %gating_ref.1, bf16[32,1024]{1,0:T(8,128)(2,1)} %cotangent_ref.1, f32[32,1024]{1,0:T(8,128)} %filters_hbm.1, f32[1,32]{1,0:T(1,128)} %bitcast.1), custom_call_target="tpu_custom_call" | custom-call | tf_op jit(solution)/shard_map/pack/pallas_call | solution.py:206
  1.9 0.0 copy-start.4
  1.9 0.0 copy-start.5
  1.9 0.0 copy-start.6
  1.9 15.5 %all_to_all.10.got_ref = bf16[32,9,2,128]{3,2,1,0:T(2,128)(2,1)S(1)} all-to-all(bf16[32,9,2,128]{3,2,1,0:T(2,128)(2,1)S(1)} %get-tuple-element.5), channel_id=1, replica_groups=mesh['ctx'=8,'chan'=4] {'ctx','chan'}, dimensions={0} | all-to-all | bytes 294912 | tf_op jit(solution)/shard_map/all_to_all | solution.py:263
  17.4 0.0 copy-done
  17.4 0.0 copy-done.4
  17.4 0.0 copy-done.5
  17.4 0.0 copy-done.6
  17.4 1.3 %spectral_products.1 = bf16[32,24,128]{2,1,0:T(8,128)(2,1)S(1)} custom-call(bf16[32,9,2,128]{3,2,1,0:T(2,128)(2,1)S(1)} %all_to_all.10.got_ref, bf16[128,256]{1,0:T(8,128)(2,1)S(1)} %copy-done.6, f32[2,64,128]{2,1,0:T(8,128)S(1)} %copy-done.5, bf16[768,256]{1,0:T(8,128)(2,1)S(1)} %copy-done, bf16[128,256]{1,0:T(8,128)(2,1)S(1)} %copy-done.4), custom_call_target="tpu_custom_call" | custom-call | tf_op jit(solution)/shard_map/spectral_products/pallas_call | solution.py:137
  18.7 0.0 copy-start.1
  18.7 0.0 copy-start.2
  18.7 0.0 copy-start.3
  18.7 10.8 %all_to_all.11.home_ref = bf16[32,24,128]{2,1,0:T(8,128)(2,1)S(1)} all-to-all(bf16[32,24,128]{2,1,0:T(8,128)(2,1)S(1)} %spectral_products.1), channel_id=1, replica_groups=mesh['ctx'=8,'chan'=4] {'ctx','chan'}, dimensions={0} | all-to-all | bytes 393216 | tf_op jit(solution)/shard_map/all_to_all | solution.py:266
  29.5 0.0 copy-done.1
  29.6 0.0 copy-done.2
  29.6 0.0 copy-done.3
  29.6 0.8 %finish.1 = (bf16[32,1024]{1,0:T(8,128)(2,1)}, bf16[32,1024]{1,0:T(8,128)(2,1)}, f32[8,1024]{1,0:T(8,128)}) custom-call(bf16[32,24,128]{2,1,0:T(8,128)(2,1)S(1)} %all_to_all.11.home_ref, bf16[32,1024]{1,0:T(8,128)(2,1)S(1)} %copy-done.1, bf16[32,1024]{1,0:T(8,128)(2,1)S(1)} %copy-done.2, bf16[32,1024]{1,0:T(8,128)(2,1)S(1)} %copy-done.3, ...), custom_call_target="tpu_custom_call" | custom-call | tf_op jit(solution)/shard_map/finish/pallas_call | solution.py:244
Async XLA Ops:
  0.6 16.8 %copy-start = (bf16[768,256]{1,0:T(8,128)(2,1)S(1)}, bf16[768,256]{1,0:T(8,128)(2,1)}, u32[]{:S(2)}) copy-start(bf16[768,256]{1,0:T(8,128)(2,1)} %constant.10.clone.second_ref) | copy-start | bytes 1179652
  1.9 15.6 %copy-start.4 = (bf16[128,256]{1,0:T(8,128)(2,1)S(1)}, bf16[128,256]{1,0:T(8,128)(2,1)}, u32[]{:S(2)}) copy-start(bf16[128,256]{1,0:T(8,128)(2,1)} %constant.11.clone.last_ref) | copy-start | bytes 196612
  1.9 15.6 %copy-start.5 = (f32[2,64,128]{2,1,0:T(8,128)S(1)}, f32[2,64,128]{2,1,0:T(8,128)}, u32[]{:S(2)}) copy-start(f32[2,64,128]{2,1,0:T(8,128)} %constant.9.clone.twiddle_ref) | copy-start | bytes 196612
  1.9 15.5 %copy-start.6 = (bf16[128,256]{1,0:T(8,128)(2,1)S(1)}, bf16[128,256]{1,0:T(8,128)(2,1)}, u32[]{:S(2)}) copy-start(bf16[128,256]{1,0:T(8,128)(2,1)} %constant.8.clone.first_ref) | copy-start | bytes 196612
  18.7 10.9 %copy-start.1 = (bf16[32,1024]{1,0:T(8,128)(2,1)S(1)}, bf16[32,1024]{1,0:T(8,128)(2,1)}, u32[]{:S(2)}) copy-start(bf16[32,1024]{1,0:T(8,128)(2,1)} %signal_ref.1) | copy-start | bytes 196612
  18.7 10.9 %copy-start.2 = (bf16[32,1024]{1,0:T(8,128)(2,1)S(1)}, bf16[32,1024]{1,0:T(8,128)(2,1)}, u32[]{:S(2)}) copy-start(bf16[32,1024]{1,0:T(8,128)(2,1)} %gating_ref.1) | copy-start | bytes 196612
  18.7 10.8 %copy-start.3 = (bf16[32,1024]{1,0:T(8,128)(2,1)S(1)}, bf16[32,1024]{1,0:T(8,128)(2,1)}, u32[]{:S(2)}) copy-start(bf16[32,1024]{1,0:T(8,128)(2,1)} %cotangent_ref.1) | copy-start | bytes 196612

commit v5 on v4

--- a/solution.py
+++ b/solution.py
@@ -27,15 +27,14 @@
     n2 = np.arange(LANES)
     outer = np.pi * (np.outer(2 * k1 + 1, n1) % (2 * height)) / height
     high, low = split_table(np.concatenate([np.cos(outer), -np.sin(outer)], axis=0))
-    first = np.concatenate([high, low, high, low], axis=1)
+    first = np.concatenate([high, low], axis=1)
     turn = np.pi * (np.outer(2 * k1 + 1, n2) % (2 * padded)) / padded
     twiddle = np.stack([np.cos(turn), np.sin(turn)]).astype(np.float32)
     inner = 2.0 * np.pi * (np.outer(n2, n2) % LANES) / LANES
     cosine, sine = np.cos(inner), np.sin(inner)
-    high, low = split_table(np.block([[cosine, -sine], [sine, cosine]]))
-    second = np.concatenate([high, high, low], axis=0)
+    second = np.block([[cosine, -sine], [sine, cosine]]).astype(jnp.bfloat16)
     high, low = split_table(np.concatenate([np.cos(outer.T), -np.sin(outer.T)], axis=1) * (2.0 / padded))
-    last = np.block([[high, high], [low, np.zeros_like(low)]])
+    last = np.concatenate([high, low], axis=0)
     return first, twiddle, second, last
 
 
@@ -49,7 +48,7 @@
 
 
 def spectral_kernel(
-    groups, peers, scale, got_ref, first_ref, twiddle_ref, second_ref, last_ref, out_ref, in_ref, part_ref, spec_ref, back_ref
+    groups, peers, scale, got_ref, first_ref, twiddle_ref, second_ref, last_ref, out_ref
 ):
     piece = out_ref.shape[1] // 3
     taps = piece // groups
@@ -62,64 +61,48 @@
         parts = [got[peer * groups + group][start : start + piece] for peer in range(peers)]
         return jnp.concatenate(parts, axis=0).astype(jnp.bfloat16)
 
-    for sequence in range(count):
-        group, start = sequence % groups, sequence // groups * piece
-        values = gather(group, start)
-        in_ref[0:rows, sequence * LANES : (sequence + 1) * LANES] = values
-        in_ref[rows : 2 * rows, sequence * LANES : (sequence + 1) * LANES] = values
-    tap_high = jnp.concatenate([part[2 * piece : 2 * piece + taps] for part in got], axis=0).astype(jnp.bfloat16)
-    tap_in = jnp.concatenate([tap_high, tap_high], axis=0)
     cosine, sine = twiddle_ref[0], twiddle_ref[1]
-    stage = dot(first_ref[:, : 2 * rows], in_ref[...])
-    tap_stage = dot(first_ref[:, : 2 * rows], tap_in)
-    total = (count + 1) * kept
-
-    def store_parts(sequence, values):
-        high, low = split(values)
-        at = slice(sequence * kept, (sequence + 1) * kept)
-        part_ref[at, : 2 * LANES] = high
-        part_ref[at, 2 * LANES : 4 * LANES] = low
-        part_ref[at, 4 * LANES :] = high
-
-    for sequence in range(count + 1):
-        source = tap_stage if sequence == count else stage[:, sequence * LANES : (sequence + 1) * LANES]
-        real, imag = source[:kept], source[kept:]
-        turned = jnp.concatenate([real * cosine + imag * sine, imag * cosine - real * sine], axis=1)
-        store_parts(sequence, turned)
-
-    def second_stage():
-        step = pl.cdiv(total, 4 * 16) * 16
-        for at in range(0, total, step):
-            stop = min(at + step, total)
-            spec_ref[at:stop] = dot(part_ref[at:stop], second_ref[...])
-
-    second_stage()
-    tap = spec_ref[count * kept : total]
-    tap_real, tap_imag = tap[:, :LANES], tap[:, LANES:]
-    corr_real = corr_imag = None
-
-    def put(sequence, real, imag):
-        store_parts(sequence, jnp.concatenate([imag, real], axis=1))
-
-    for group in range(groups):
-        sig = spec_ref[group * kept : (group + 1) * kept]
-        gat = spec_ref[(groups + group) * kept : (groups + group + 1) * kept]
-        sr, si, gr, gi = sig[:, :LANES], sig[:, LANES:], gat[:, :LANES], gat[:, LANES:]
-        put(group, sr * tap_real - si * tap_imag, sr * tap_imag + si * tap_real)
-        put(groups + group, tap_real * gr + tap_imag * gi, tap_real * gi - tap_imag * gr)
-        cr, ci = sr * gr + si * gi, sr * gi - si * gr
-        corr_real, corr_imag = (cr, ci) if corr_real is None else (corr_real + cr, corr_imag + ci)
-    put(count, corr_real * scale, corr_imag * scale)
-    second_stage()
-    for sequence in range(count + 1):
-        both = spec_ref[sequence * kept : (sequence + 1) * kept]
-        imag, real = both[:, :LANES], both[:, LANES:]
-        turned = jnp.concatenate([real * cosine - imag * sine, imag * cosine + real * sine], axis=0)
-        high, low = split(turned)
-        back_ref[: 2 * kept, sequence * LANES : (sequence + 1) * LANES] = high
-        back_ref[2 * kept :, sequence * LANES : (sequence + 1) * LANES] = low
-    both = dot(last_ref[...], back_ref[...])
-    result = both[:rows] + both[rows:]
+    second = second_ref[...]
+
+    def first_stage(values):
+        return dot(first_ref[...], jnp.concatenate([values, values], axis=0))
+
+    def turn_forward(stage):
+        parts = []
+        for at in range(0, stage.shape[1], LANES):
+            real, imag = stage[:kept, at : at + LANES], stage[kept:, at : at + LANES]
+            turned = jnp.concatenate([real * cosine + imag * sine, imag * cosine - real * sine], axis=1)
+            parts.append(turned.astype(jnp.bfloat16))
+        return parts
+
+    def second_stage(parts):
+        both = dot(jnp.concatenate(parts, axis=0), second)
+        cuts = [both[at : at + kept] for at in range(0, both.shape[0], kept)]
+        return [(cut[:, :LANES], cut[:, LANES:]) for cut in cuts]
+
+    def swapped(real, imag):
+        return jnp.concatenate([imag, real], axis=1).astype(jnp.bfloat16)
+
+    def last_stage(swapped_pairs):
+        parts = []
+        for imag, real in swapped_pairs:
+            turned = jnp.concatenate([real * cosine - imag * sine, imag * cosine + real * sine], axis=0)
+            parts.append(turned.astype(jnp.bfloat16))
+        both = dot(last_ref[...], jnp.concatenate(parts, axis=1))
+        return both[:rows] + both[rows:]
+
+    taps_in = jnp.concatenate([part[2 * piece : 2 * piece + taps] for part in got], axis=0).astype(jnp.bfloat16)
+    signal_in = jnp.concatenate([gather(group, 0) for group in range(groups)] + [taps_in], axis=1)
+    grad_in = jnp.concatenate([gather(group, piece) for group in range(groups)], axis=1)
+    signal_stage = first_stage(signal_in)
+    grad_stage = first_stage(grad_in)
+    forward = second_stage(turn_forward(signal_stage) + turn_forward(grad_stage))
+    signals, (tap_real, tap_imag), grads = forward[:groups], forward[groups], forward[groups + 1 :]
+    conv_parts = [swapped(r * tap_real - i * tap_imag, r * tap_imag + i * tap_real) for r, i in signals]
+    back_parts = [swapped(tap_real * r + tap_imag * i, tap_real * i - tap_imag * r) for r, i in grads]
+    corr_real = sum(sr * gr + si * gi for (sr, si), (gr, gi) in zip(signals, grads)) * scale
+    corr_imag = sum(sr * gi - si * gr for (sr, si), (gr, gi) in zip(signals, grads)) * scale
+    result = last_stage(second_stage(conv_parts + back_parts + [swapped(corr_real, corr_imag)]))
     for peer in range(peers):
         piece_rows = result[peer * piece : (peer + 1) * piece]
         for group in range(groups):
@@ -131,20 +114,12 @@
 def spectral_products(got, piece, groups, peers, scale):
     rows = peers * piece
     tables = dft_tables(rows)
-    kept = tables[1].shape[1]
-    total = (2 * groups + 1) * kept
     vmem = pl.BlockSpec(memory_space=pltpu.VMEM)
     return pl.pallas_call(
         functools.partial(spectral_kernel, groups, peers, scale),
         out_shape=jax.ShapeDtypeStruct((got.shape[0], 3 * piece, LANES), jnp.bfloat16),
         in_specs=[vmem] * 5,
         out_specs=vmem,
-        scratch_shapes=[
-            pltpu.VMEM((2 * rows, 2 * groups * LANES), jnp.bfloat16),
-            pltpu.VMEM((total, 6 * LANES), jnp.bfloat16),
-            pltpu.VMEM((total, 2 * LANES), jnp.float32),
-            pltpu.VMEM((4 * kept, (2 * groups + 1) * LANES), jnp.bfloat16),
-        ],
         compiler_params=pltpu.CompilerParams(vmem_limit_bytes=24 * 2**20),
         name="spectral_products",
     )(got, *[jnp.asarray(table) for table in tables])

time: 30.7 us -> 30.2 us (0.984)
  Pallas kernels: 3.21 us -> 2.7 us
    pallas_call x1, Pallas kernels: 1.25 us -> 0.79 us  [spectral_products(): pl.pallas_call(functools.partial(spectral_kernel, groups, peers, scale),...]
where the time goes in v5:
time: 30.2 us; the launch traced here: 29.8 us
  blocking collectives  26.3 us (87%)
  Pallas kernels  2.7 us (9%)
  between operations  0.72 us (2%)
    all_to_all x1, blocking collectives, filter_per_device(): lax.all_to_all(message, both_axes, split_axis=0, concat_axis=0, tiled=True)  15.5 us
    all_to_all x1, blocking collectives, filter_per_device(): lax.all_to_all(result, both_axes, split_axis=0, concat_axis=0, tiled=True)  10.8 us
    pallas_call x1, Pallas kernels, pack(): pl.pallas_call(functools.partial(pack_kernel, groups), out_shape=(jax.Sha...  1.15 us
    pallas_call x1, Pallas kernels, spectral_products(): pl.pallas_call(functools.partial(spectral_kernel, groups, peers, scale),...  0.79 us
    pallas_call x1, Pallas kernels, finish(): pl.pallas_call(functools.partial(finish_kernel, groups), out_shape=(jax.S...  0.76 us

profile of v5, /device:TPU:0, one launch (start us, length us, event | category | flops | bytes accessed | tf_op | source)
XLA Modules:
  0.0 29.8 jit_solution(10348984493751689687)
XLA Ops:
  0.6 1.2 %pack.1 = (bf16[32,9,2,128]{3,2,1,0:T(2,128)(2,1)S(1)}, f32[32,128]{1,0:T(8,128)S(1)}) custom-call(bf16[32,1024]{1,0:T(8,128)(2,1)} %signal_ref.1, bf16[32,1024]{1,0:T(8,128)(2,1)} %gating_ref.1, bf16[32,1024]{1,0:T(8,128)(2,1)} %cotangent_ref.1, f32[32,1024]{1,0:T(8,128)} %filters_hbm.1, f32[1,32]{1,0:T(1,128)} %bitcast.1), custom_call_target="tpu_custom_call" | custom-call | tf_op jit(solution)/shard_map/pack/pallas_call | solution.py:181
  1.8 0.0 copy-start.3
  1.8 0.0 copy-start.4
  1.8 0.0 copy-start.5
  1.8 0.0 copy-start.6
  1.8 15.5 %all_to_all.10.got_ref = bf16[32,9,2,128]{3,2,1,0:T(2,128)(2,1)S(1)} all-to-all(bf16[32,9,2,128]{3,2,1,0:T(2,128)(2,1)S(1)} %get-tuple-element.5), channel_id=1, replica_groups=mesh['ctx'=8,'chan'=4] {'ctx','chan'}, dimensions={0} | all-to-all | bytes 294912 | tf_op jit(solution)/shard_map/all_to_all | solution.py:238
  17.4 0.0 copy-done.3
  17.4 0.0 copy-done.4
  17.4 0.0 copy-done.5
  17.4 0.0 copy-done.6
  17.4 0.8 %spectral_products.1 = bf16[32,24,128]{2,1,0:T(8,128)(2,1)S(1)} custom-call(bf16[32,9,2,128]{3,2,1,0:T(2,128)(2,1)S(1)} %all_to_all.10.got_ref, bf16[128,128]{1,0:T(8,128)(2,1)S(1)} %copy-done.6, f32[2,64,128]{2,1,0:T(8,128)S(1)} %copy-done.4, bf16[256,256]{1,0:T(8,128)(2,1)S(1)} %copy-done.3, bf16[128,128]{1,0:T(8,128)(2,1)S(1)} %copy-done.5), custom_call_target="tpu_custom_call" | custom-call | tf_op jit(solution)/shard_map/spectral_products/pallas_call | solution.py:118
  18.2 0.0 copy-start
  18.2 0.0 copy-start.1
  18.2 0.0 copy-start.2
  18.2 10.8 %all_to_all.11.home_ref = bf16[32,24,128]{2,1,0:T(8,128)(2,1)S(1)} all-to-all(bf16[32,24,128]{2,1,0:T(8,128)(2,1)S(1)} %spectral_products.1), channel_id=1, replica_groups=mesh['ctx'=8,'chan'=4] {'ctx','chan'}, dimensions={0} | all-to-all | bytes 393216 | tf_op jit(solution)/shard_map/all_to_all | solution.py:241
  29.0 0.0 copy-done
  29.0 0.0 copy-done.1
  29.0 0.0 copy-done.2
  29.0 0.8 %finish.1 = (bf16[32,1024]{1,0:T(8,128)(2,1)}, bf16[32,1024]{1,0:T(8,128)(2,1)}, f32[8,1024]{1,0:T(8,128)}) custom-call(bf16[32,24,128]{2,1,0:T(8,128)(2,1)S(1)} %all_to_all.11.home_ref, bf16[32,1024]{1,0:T(8,128)(2,1)S(1)} %copy-done, bf16[32,1024]{1,0:T(8,128)(2,1)S(1)} %copy-done.1, bf16[32,1024]{1,0:T(8,128)(2,1)S(1)} %copy-done.2, ...), custom_call_target="tpu_custom_call" | custom-call | tf_op jit(solution)/shard_map/finish/pallas_call | solution.py:219
Async XLA Ops:
  1.8 15.6 %copy-start.3 = (bf16[256,256]{1,0:T(8,128)(2,1)S(1)}, bf16[256,256]{1,0:T(8,128)(2,1)}, u32[]{:S(2)}) copy-start(bf16[256,256]{1,0:T(8,128)(2,1)} %constant.10.clone.second_ref) | copy-start | bytes 393220
  1.8 15.6 %copy-start.4 = (f32[2,64,128]{2,1,0:T(8,128)S(1)}, f32[2,64,128]{2,1,0:T(8,128)}, u32[]{:S(2)}) copy-start(f32[2,64,128]{2,1,0:T(8,128)} %constant.9.clone.twiddle_ref) | copy-start | bytes 196612
  1.8 15.6 %copy-start.5 = (bf16[128,128]{1,0:T(8,128)(2,1)S(1)}, bf16[128,128]{1,0:T(8,128)(2,1)}, u32[]{:S(2)}) copy-start(bf16[128,128]{1,0:T(8,128)(2,1)} %constant.11.clone.last_ref) | copy-start | bytes 98308
  1.8 15.5 %copy-start.6 = (bf16[128,128]{1,0:T(8,128)(2,1)S(1)}, bf16[128,128]{1,0:T(8,128)(2,1)}, u32[]{:S(2)}) copy-start(bf16[128,128]{1,0:T(8,128)(2,1)} %constant.8.clone.first_ref) | copy-start | bytes 98308
  18.2 10.9 %copy-start = (bf16[32,1024]{1,0:T(8,128)(2,1)S(1)}, bf16[32,1024]{1,0:T(8,128)(2,1)}, u32[]{:S(2)}) copy-start(bf16[32,1024]{1,0:T(8,128)(2,1)} %signal_ref.1) | copy-start | bytes 196612
  18.2 10.9 %copy-start.1 = (bf16[32,1024]{1,0:T(8,128)(2,1)S(1)}, bf16[32,1024]{1,0:T(8,128)(2,1)}, u32[]{:S(2)}) copy-start(bf16[32,1024]{1,0:T(8,128)(2,1)} %gating_ref.1) | copy-start | bytes 196612
  18.2 10.8 %copy-start.2 = (bf16[32,1024]{1,0:T(8,128)(2,1)S(1)}, bf16[32,1024]{1,0:T(8,128)(2,1)}, u32[]{:S(2)}) copy-start(bf16[32,1024]{1,0:T(8,128)(2,1)} %cotangent_ref.1) | copy-start | bytes 196612

commit v6 on v5

--- a/solution.py
+++ b/solution.py
@@ -47,6 +47,18 @@
     return high, (values - high.astype(jnp.float32)).astype(jnp.bfloat16)
 
 
+def slot_order(peers, groups):
+    if peers % 2 or groups % 2:
+        return list(range(peers * groups))
+    return [
+        (high * 2 + low) * groups + (plane * 2 + core)
+        for plane in range(groups // 2)
+        for low in range(2)
+        for high in reversed(range(peers // 2))
+        for core in range(2)
+    ]
+
+
 def spectral_kernel(
     groups, peers, scale, got_ref, first_ref, twiddle_ref, second_ref, last_ref, out_ref
 ):
@@ -55,7 +67,10 @@
     rows = peers * piece
     kept = twiddle_ref.shape[1]
     count = 2 * groups
+    order = slot_order(peers, groups)
+    slots = [order.index(device) for device in range(peers * groups)]
     got = got_ref[...].astype(jnp.float32).reshape(peers * groups, -1, LANES)
+    got = [got[slot] for slot in slots]
 
     def gather(group, start):
         parts = [got[peer * groups + group][start : start + piece] for peer in range(peers)]
@@ -108,7 +123,7 @@
         for group in range(groups):
             cut = lambda sequence: piece_rows[:, sequence * LANES : (sequence + 1) * LANES]
             message = jnp.concatenate([cut(group), cut(groups + group), cut(count)], axis=0)
-            out_ref[peer * groups + group] = message.astype(jnp.bfloat16)
+            out_ref[slots[peer * groups + group]] = message.astype(jnp.bfloat16)
 
 
 def spectral_products(got, piece, groups, peers, scale):
@@ -233,12 +248,19 @@
 def filter_per_device(signal, gating, cotangent, filters, skip_weight):
     peers = lax.axis_size("ctx")
     groups = lax.axis_size("chan")
-    both_axes = ("ctx", "chan")
     message, column = pack(signal, gating, cotangent, filters, skip_weight, groups)
-    got = lax.all_to_all(message, both_axes, split_axis=0, concat_axis=0, tiled=True)
+    exchange = functools.partial(
+        lax.all_to_all,
+        axis_name=("ctx", "chan"),
+        split_axis=0,
+        concat_axis=0,
+        axis_index_groups=[slot_order(peers, groups)],
+        tiled=True,
+    )
+    got = exchange(message)
     scale = 1.0 / math.sqrt(signal.shape[1] * peers * groups)
     result = spectral_products(got, signal.shape[1] // LANES, groups, peers, scale)
-    home = lax.all_to_all(result, both_axes, split_axis=0, concat_axis=0, tiled=True)
+    home = exchange(result)
     return finish(home, signal, gating, cotangent, column, groups)
 
 

time: 30.2 us -> 29.9 us (0.990)
  no operation moved by 1% of the time
where the time goes in v6:
time: 29.9 us; the launch traced here: 29.6 us
  blocking collectives  26.2 us (88%)
  Pallas kernels  2.7 us (9%)
  between operations  0.72 us (2%)
    all_to_all x1, blocking collectives, filter_per_device(): got = exchange(message)  15.3 us
    all_to_all x1, blocking collectives, filter_per_device(): home = exchange(result)  10.9 us
    pallas_call x1, Pallas kernels, pack(): pl.pallas_call(functools.partial(pack_kernel, groups), out_shape=(jax.Sha...  1.15 us
    pallas_call x1, Pallas kernels, spectral_products(): pl.pallas_call(functools.partial(spectral_kernel, groups, peers, scale),...  0.79 us
    pallas_call x1, Pallas kernels, finish(): pl.pallas_call(functools.partial(finish_kernel, groups), out_shape=(jax.S...  0.76 us

profile of v6, /device:TPU:0, one launch (start us, length us, event | category | flops | bytes accessed | tf_op | source)
XLA Modules:
  0.0 29.6 jit_solution(15329430430829587584)
XLA Ops:
  0.6 1.2 %pack.1 = (bf16[32,9,2,128]{3,2,1,0:T(2,128)(2,1)S(1)}, f32[32,128]{1,0:T(8,128)S(1)}) custom-call(bf16[32,1024]{1,0:T(8,128)(2,1)} %signal_ref.1, bf16[32,1024]{1,0:T(8,128)(2,1)} %gating_ref.1, bf16[32,1024]{1,0:T(8,128)(2,1)} %cotangent_ref.1, f32[32,1024]{1,0:T(8,128)} %filters_hbm.1, f32[1,32]{1,0:T(1,128)} %bitcast.1), custom_call_target="tpu_custom_call" | custom-call | tf_op jit(solution)/shard_map/pack/pallas_call | solution.py:196
  1.8 0.0 copy-start.3
  1.8 0.0 copy-start.4
  1.8 0.0 copy-start.5
  1.8 0.0 copy-start.6
  1.8 15.3 %all_to_all.10.got_ref = bf16[32,9,2,128]{3,2,1,0:T(2,128)(2,1)S(1)} all-to-all(bf16[32,9,2,128]{3,2,1,0:T(2,128)(2,1)S(1)} %get-tuple-element.5), channel_id=1, replica_groups={{24,25,16,17,8,9,0,1,28,29,20,21,12,13,4,5,26,27,18,19,10,11,2,3,30,31,..., dimensions={0} | all-to-all | bytes 294912 | tf_op jit(solution)/shard_map/all_to_all | solution.py:260
  17.1 0.0 copy-done.3
  17.1 0.0 copy-done.4
  17.1 0.0 copy-done.5
  17.1 0.0 copy-done.6
  17.1 0.8 %spectral_products.1 = bf16[32,24,128]{2,1,0:T(8,128)(2,1)S(1)} custom-call(bf16[32,9,2,128]{3,2,1,0:T(2,128)(2,1)S(1)} %all_to_all.10.got_ref, bf16[128,128]{1,0:T(8,128)(2,1)S(1)} %copy-done.6, f32[2,64,128]{2,1,0:T(8,128)S(1)} %copy-done.4, bf16[256,256]{1,0:T(8,128)(2,1)S(1)} %copy-done.3, bf16[128,128]{1,0:T(8,128)(2,1)S(1)} %copy-done.5), custom_call_target="tpu_custom_call" | custom-call | tf_op jit(solution)/shard_map/spectral_products/pallas_call | solution.py:133
  17.9 0.0 copy-start
  17.9 0.0 copy-start.1
  17.9 0.0 copy-start.2
  18.0 10.9 %all_to_all.11.home_ref = bf16[32,24,128]{2,1,0:T(8,128)(2,1)S(1)} all-to-all(bf16[32,24,128]{2,1,0:T(8,128)(2,1)S(1)} %spectral_products.1), channel_id=1, replica_groups={{24,25,16,17,8,9,0,1,28,29,20,21,12,13,4,5,26,27,18,19,10,11,2,3,30,31,..., dimensions={0} | all-to-all | bytes 393216 | tf_op jit(solution)/shard_map/all_to_all | solution.py:263
  28.9 0.0 copy-done
  28.9 0.0 copy-done.1
  28.9 0.0 copy-done.2
  28.9 0.8 %finish.1 = (bf16[32,1024]{1,0:T(8,128)(2,1)}, bf16[32,1024]{1,0:T(8,128)(2,1)}, f32[8,1024]{1,0:T(8,128)}) custom-call(bf16[32,24,128]{2,1,0:T(8,128)(2,1)S(1)} %all_to_all.11.home_ref, bf16[32,1024]{1,0:T(8,128)(2,1)S(1)} %copy-done, bf16[32,1024]{1,0:T(8,128)(2,1)S(1)} %copy-done.1, bf16[32,1024]{1,0:T(8,128)(2,1)S(1)} %copy-done.2, ...), custom_call_target="tpu_custom_call" | custom-call | tf_op jit(solution)/shard_map/finish/pallas_call | solution.py:234
Async XLA Ops:
  1.8 15.3 %copy-start.3 = (bf16[256,256]{1,0:T(8,128)(2,1)S(1)}, bf16[256,256]{1,0:T(8,128)(2,1)}, u32[]{:S(2)}) copy-start(bf16[256,256]{1,0:T(8,128)(2,1)} %constant.10.clone.second_ref) | copy-start | bytes 393220
  1.8 15.3 %copy-start.4 = (f32[2,64,128]{2,1,0:T(8,128)S(1)}, f32[2,64,128]{2,1,0:T(8,128)}, u32[]{:S(2)}) copy-start(f32[2,64,128]{2,1,0:T(8,128)} %constant.9.clone.twiddle_ref) | copy-start | bytes 196612
  1.8 15.3 %copy-start.5 = (bf16[128,128]{1,0:T(8,128)(2,1)S(1)}, bf16[128,128]{1,0:T(8,128)(2,1)}, u32[]{:S(2)}) copy-start(bf16[128,128]{1,0:T(8,128)(2,1)} %constant.11.clone.last_ref) | copy-start | bytes 98308
  1.8 15.3 %copy-start.6 = (bf16[128,128]{1,0:T(8,128)(2,1)S(1)}, bf16[128,128]{1,0:T(8,128)(2,1)}, u32[]{:S(2)}) copy-start(bf16[128,128]{1,0:T(8,128)(2,1)} %constant.8.clone.first_ref) | copy-start | bytes 98308
  17.9 11.0 %copy-start = (bf16[32,1024]{1,0:T(8,128)(2,1)S(1)}, bf16[32,1024]{1,0:T(8,128)(2,1)}, u32[]{:S(2)}) copy-start(bf16[32,1024]{1,0:T(8,128)(2,1)} %signal_ref.1) | copy-start | bytes 196612
  17.9 10.9 %copy-start.1 = (bf16[32,1024]{1,0:T(8,128)(2,1)S(1)}, bf16[32,1024]{1,0:T(8,128)(2,1)}, u32[]{:S(2)}) copy-start(bf16[32,1024]{1,0:T(8,128)(2,1)} %gating_ref.1) | copy-start | bytes 196612
  17.9 10.9 %copy-start.2 = (bf16[32,1024]{1,0:T(8,128)(2,1)S(1)}, bf16[32,1024]{1,0:T(8,128)(2,1)}, u32[]{:S(2)}) copy-start(bf16[32,1024]{1,0:T(8,128)(2,1)} %cotangent_ref.1) | copy-start | bytes 196612

commit v7 on v6

--- a/solution.py
+++ b/solution.py
@@ -42,18 +42,13 @@
     return jnp.dot(left, right, preferred_element_type=jnp.float32)
 
 
-def split(values):
-    high = values.astype(jnp.bfloat16)
-    return high, (values - high.astype(jnp.float32)).astype(jnp.bfloat16)
-
-
 def slot_order(peers, groups):
     if peers % 2 or groups % 2:
         return list(range(peers * groups))
     return [
         (high * 2 + low) * groups + (plane * 2 + core)
         for plane in range(groups // 2)
-        for low in range(2)
+        for low in reversed(range(2))
         for high in reversed(range(peers // 2))
         for core in range(2)
     ]

time: 29.9 us -> 29.8 us (level)
  no operation moved by 1% of the time
where the time goes in v7:
time: 29.8 us; the launch traced here: 29.4 us
  blocking collectives  26 us (87%)
  Pallas kernels  2.7 us (9%)
  between operations  0.72 us (2%)
    all_to_all x1, blocking collectives, filter_per_device(): got = exchange(message)  15 us
    all_to_all x1, blocking collectives, filter_per_device(): home = exchange(result)  10.9 us
    pallas_call x1, Pallas kernels, pack(): pl.pallas_call(functools.partial(pack_kernel, groups), out_shape=(jax.Sha...  1.15 us
    pallas_call x1, Pallas kernels, spectral_products(): pl.pallas_call(functools.partial(spectral_kernel, groups, peers, scale),...  0.79 us
    pallas_call x1, Pallas kernels, finish(): pl.pallas_call(functools.partial(finish_kernel, groups), out_shape=(jax.S...  0.76 us

profile of v7, /device:TPU:0, one launch (start us, length us, event | category | flops | bytes accessed | tf_op | source)
XLA Modules:
  0.0 29.4 jit_solution(17346862770364773861)
XLA Ops:
  0.6 1.2 %pack.1 = (bf16[32,9,2,128]{3,2,1,0:T(2,128)(2,1)S(1)}, f32[32,128]{1,0:T(8,128)S(1)}) custom-call(bf16[32,1024]{1,0:T(8,128)(2,1)} %signal_ref.1, bf16[32,1024]{1,0:T(8,128)(2,1)} %gating_ref.1, bf16[32,1024]{1,0:T(8,128)(2,1)} %cotangent_ref.1, f32[32,1024]{1,0:T(8,128)} %filters_hbm.1, f32[1,32]{1,0:T(1,128)} %bitcast.1), custom_call_target="tpu_custom_call" | custom-call | tf_op jit(solution)/shard_map/pack/pallas_call | solution.py:191
  1.8 0.0 copy-start.3
  1.8 0.0 copy-start.4
  1.8 0.0 copy-start.5
  1.8 0.0 copy-start.6
  1.8 15.0 %all_to_all.10.got_ref = bf16[32,9,2,128]{3,2,1,0:T(2,128)(2,1)S(1)} all-to-all(bf16[32,9,2,128]{3,2,1,0:T(2,128)(2,1)S(1)} %get-tuple-element.5), channel_id=1, replica_groups={{28,29,20,21,12,13,4,5,24,25,16,17,8,9,0,1,30,31,22,23,14,15,6,7,26,27,..., dimensions={0} | all-to-all | bytes 294912 | tf_op jit(solution)/shard_map/all_to_all | solution.py:255
  16.9 0.0 copy-done.3
  16.9 0.0 copy-done.4
  16.9 0.0 copy-done.5
  16.9 0.0 copy-done.6
  16.9 0.8 %spectral_products.1 = bf16[32,24,128]{2,1,0:T(8,128)(2,1)S(1)} custom-call(bf16[32,9,2,128]{3,2,1,0:T(2,128)(2,1)S(1)} %all_to_all.10.got_ref, bf16[128,128]{1,0:T(8,128)(2,1)S(1)} %copy-done.6, f32[2,64,128]{2,1,0:T(8,128)S(1)} %copy-done.4, bf16[256,256]{1,0:T(8,128)(2,1)S(1)} %copy-done.3, bf16[128,128]{1,0:T(8,128)(2,1)S(1)} %copy-done.5), custom_call_target="tpu_custom_call" | custom-call | tf_op jit(solution)/shard_map/spectral_products/pallas_call | solution.py:128
  17.7 0.0 copy-start
  17.7 0.0 copy-start.1
  17.7 0.0 copy-start.2
  17.7 10.9 %all_to_all.11.home_ref = bf16[32,24,128]{2,1,0:T(8,128)(2,1)S(1)} all-to-all(bf16[32,24,128]{2,1,0:T(8,128)(2,1)S(1)} %spectral_products.1), channel_id=1, replica_groups={{28,29,20,21,12,13,4,5,24,25,16,17,8,9,0,1,30,31,22,23,14,15,6,7,26,27,..., dimensions={0} | all-to-all | bytes 393216 | tf_op jit(solution)/shard_map/all_to_all | solution.py:258
  28.6 0.0 copy-done
  28.6 0.0 copy-done.1
  28.7 0.0 copy-done.2
  28.7 0.8 %finish.1 = (bf16[32,1024]{1,0:T(8,128)(2,1)}, bf16[32,1024]{1,0:T(8,128)(2,1)}, f32[8,1024]{1,0:T(8,128)}) custom-call(bf16[32,24,128]{2,1,0:T(8,128)(2,1)S(1)} %all_to_all.11.home_ref, bf16[32,1024]{1,0:T(8,128)(2,1)S(1)} %copy-done, bf16[32,1024]{1,0:T(8,128)(2,1)S(1)} %copy-done.1, bf16[32,1024]{1,0:T(8,128)(2,1)S(1)} %copy-done.2, ...), custom_call_target="tpu_custom_call" | custom-call | tf_op jit(solution)/shard_map/finish/pallas_call | solution.py:229
Async XLA Ops:
  1.8 15.1 %copy-start.3 = (bf16[256,256]{1,0:T(8,128)(2,1)S(1)}, bf16[256,256]{1,0:T(8,128)(2,1)}, u32[]{:S(2)}) copy-start(bf16[256,256]{1,0:T(8,128)(2,1)} %constant.10.clone.second_ref) | copy-start | bytes 393220
  1.8 15.1 %copy-start.4 = (f32[2,64,128]{2,1,0:T(8,128)S(1)}, f32[2,64,128]{2,1,0:T(8,128)}, u32[]{:S(2)}) copy-start(f32[2,64,128]{2,1,0:T(8,128)} %constant.9.clone.twiddle_ref) | copy-start | bytes 196612
  1.8 15.1 %copy-start.5 = (bf16[128,128]{1,0:T(8,128)(2,1)S(1)}, bf16[128,128]{1,0:T(8,128)(2,1)}, u32[]{:S(2)}) copy-start(bf16[128,128]{1,0:T(8,128)(2,1)} %constant.11.clone.last_ref) | copy-start | bytes 98308
  1.8 15.1 %copy-start.6 = (bf16[128,128]{1,0:T(8,128)(2,1)S(1)}, bf16[128,128]{1,0:T(8,128)(2,1)}, u32[]{:S(2)}) copy-start(bf16[128,128]{1,0:T(8,128)(2,1)} %constant.8.clone.first_ref) | copy-start | bytes 98308
  17.7 11.0 %copy-start = (bf16[32,1024]{1,0:T(8,128)(2,1)S(1)}, bf16[32,1024]{1,0:T(8,128)(2,1)}, u32[]{:S(2)}) copy-start(bf16[32,1024]{1,0:T(8,128)(2,1)} %signal_ref.1) | copy-start | bytes 196612
  17.7 11.0 %copy-start.1 = (bf16[32,1024]{1,0:T(8,128)(2,1)S(1)}, bf16[32,1024]{1,0:T(8,128)(2,1)}, u32[]{:S(2)}) copy-start(bf16[32,1024]{1,0:T(8,128)(2,1)} %gating_ref.1) | copy-start | bytes 196612
  17.7 10.9 %copy-start.2 = (bf16[32,1024]{1,0:T(8,128)(2,1)S(1)}, bf16[32,1024]{1,0:T(8,128)(2,1)}, u32[]{:S(2)}) copy-start(bf16[32,1024]{1,0:T(8,128)(2,1)} %cotangent_ref.1) | copy-start | bytes 196612

commit v8 on v7

--- a/solution.py
+++ b/solution.py
@@ -48,8 +48,8 @@
     return [
         (high * 2 + low) * groups + (plane * 2 + core)
         for plane in range(groups // 2)
-        for low in reversed(range(2))
-        for high in reversed(range(peers // 2))
+        for low in range(2)
+        for high in [0, *reversed(range(1, peers // 2))]
         for core in range(2)
     ]
 

time: 29.8 us -> 29.6 us (level)
  no operation moved by 1% of the time
where the time goes in v8:
time: 29.6 us; the launch traced here: 29.4 us
  blocking collectives  25.9 us (88%)
  Pallas kernels  2.7 us (9%)
  between operations  0.72 us (2%)
    all_to_all x1, blocking collectives, filter_per_device(): got = exchange(message)  15.1 us
    all_to_all x1, blocking collectives, filter_per_device(): home = exchange(result)  10.9 us
    pallas_call x1, Pallas kernels, pack(): pl.pallas_call(functools.partial(pack_kernel, groups), out_shape=(jax.Sha...  1.15 us
    pallas_call x1, Pallas kernels, spectral_products(): pl.pallas_call(functools.partial(spectral_kernel, groups, peers, scale),...  0.79 us
    pallas_call x1, Pallas kernels, finish(): pl.pallas_call(functools.partial(finish_kernel, groups), out_shape=(jax.S...  0.76 us

profile of v8, /device:TPU:0, one launch (start us, length us, event | category | flops | bytes accessed | tf_op | source)
XLA Modules:
  0.0 29.4 jit_solution(7223224241134933550)
XLA Ops:
  0.6 1.2 %pack.1 = (bf16[32,9,2,128]{3,2,1,0:T(2,128)(2,1)S(1)}, f32[32,128]{1,0:T(8,128)S(1)}) custom-call(bf16[32,1024]{1,0:T(8,128)(2,1)} %signal_ref.1, bf16[32,1024]{1,0:T(8,128)(2,1)} %gating_ref.1, bf16[32,1024]{1,0:T(8,128)(2,1)} %cotangent_ref.1, f32[32,1024]{1,0:T(8,128)} %filters_hbm.1, f32[1,32]{1,0:T(1,128)} %bitcast.1), custom_call_target="tpu_custom_call" | custom-call | tf_op jit(solution)/shard_map/pack/pallas_call | solution.py:191
  1.8 0.0 copy-start.3
  1.8 0.0 copy-start.4
  1.8 0.0 copy-start.5
  1.8 0.0 copy-start.6
  1.8 15.1 %all_to_all.10.got_ref = bf16[32,9,2,128]{3,2,1,0:T(2,128)(2,1)S(1)} all-to-all(bf16[32,9,2,128]{3,2,1,0:T(2,128)(2,1)S(1)} %get-tuple-element.5), channel_id=1, replica_groups={{0,1,24,25,16,17,8,9,4,5,28,29,20,21,12,13,2,3,26,27,18,19,10,11,6,7,30..., dimensions={0} | all-to-all | bytes 294912 | tf_op jit(solution)/shard_map/all_to_all | solution.py:255
  16.9 0.0 copy-done.3
  16.9 0.0 copy-done.4
  16.9 0.0 copy-done.5
  16.9 0.0 copy-done.6
  16.9 0.8 %spectral_products.1 = bf16[32,24,128]{2,1,0:T(8,128)(2,1)S(1)} custom-call(bf16[32,9,2,128]{3,2,1,0:T(2,128)(2,1)S(1)} %all_to_all.10.got_ref, bf16[128,128]{1,0:T(8,128)(2,1)S(1)} %copy-done.6, f32[2,64,128]{2,1,0:T(8,128)S(1)} %copy-done.4, bf16[256,256]{1,0:T(8,128)(2,1)S(1)} %copy-done.3, bf16[128,128]{1,0:T(8,128)(2,1)S(1)} %copy-done.5), custom_call_target="tpu_custom_call" | custom-call | tf_op jit(solution)/shard_map/spectral_products/pallas_call | solution.py:128
  17.7 0.0 copy-start
  17.7 0.0 copy-start.1
  17.7 0.0 copy-start.2
  17.8 10.9 %all_to_all.11.home_ref = bf16[32,24,128]{2,1,0:T(8,128)(2,1)S(1)} all-to-all(bf16[32,24,128]{2,1,0:T(8,128)(2,1)S(1)} %spectral_products.1), channel_id=1, replica_groups={{0,1,24,25,16,17,8,9,4,5,28,29,20,21,12,13,2,3,26,27,18,19,10,11,6,7,30..., dimensions={0} | all-to-all | bytes 393216 | tf_op jit(solution)/shard_map/all_to_all | solution.py:258
  28.6 0.0 copy-done
  28.6 0.0 copy-done.1
  28.6 0.0 copy-done.2
  28.6 0.8 %finish.1 = (bf16[32,1024]{1,0:T(8,128)(2,1)}, bf16[32,1024]{1,0:T(8,128)(2,1)}, f32[8,1024]{1,0:T(8,128)}) custom-call(bf16[32,24,128]{2,1,0:T(8,128)(2,1)S(1)} %all_to_all.11.home_ref, bf16[32,1024]{1,0:T(8,128)(2,1)S(1)} %copy-done, bf16[32,1024]{1,0:T(8,128)(2,1)S(1)} %copy-done.1, bf16[32,1024]{1,0:T(8,128)(2,1)S(1)} %copy-done.2, ...), custom_call_target="tpu_custom_call" | custom-call | tf_op jit(solution)/shard_map/finish/pallas_call | solution.py:229
Async XLA Ops:
  1.8 15.1 %copy-start.3 = (bf16[256,256]{1,0:T(8,128)(2,1)S(1)}, bf16[256,256]{1,0:T(8,128)(2,1)}, u32[]{:S(2)}) copy-start(bf16[256,256]{1,0:T(8,128)(2,1)} %constant.10.clone.second_ref) | copy-start | bytes 393220
  1.8 15.1 %copy-start.4 = (f32[2,64,128]{2,1,0:T(8,128)S(1)}, f32[2,64,128]{2,1,0:T(8,128)}, u32[]{:S(2)}) copy-start(f32[2,64,128]{2,1,0:T(8,128)} %constant.9.clone.twiddle_ref) | copy-start | bytes 196612
  1.8 15.1 %copy-start.5 = (bf16[128,128]{1,0:T(8,128)(2,1)S(1)}, bf16[128,128]{1,0:T(8,128)(2,1)}, u32[]{:S(2)}) copy-start(bf16[128,128]{1,0:T(8,128)(2,1)} %constant.11.clone.last_ref) | copy-start | bytes 98308
  1.8 15.1 %copy-start.6 = (bf16[128,128]{1,0:T(8,128)(2,1)S(1)}, bf16[128,128]{1,0:T(8,128)(2,1)}, u32[]{:S(2)}) copy-start(bf16[128,128]{1,0:T(8,128)(2,1)} %constant.8.clone.first_ref) | copy-start | bytes 98308
  17.7 10.9 %copy-start = (bf16[32,1024]{1,0:T(8,128)(2,1)S(1)}, bf16[32,1024]{1,0:T(8,128)(2,1)}, u32[]{:S(2)}) copy-start(bf16[32,1024]{1,0:T(8,128)(2,1)} %signal_ref.1) | copy-start | bytes 196612
  17.7 10.9 %copy-start.1 = (bf16[32,1024]{1,0:T(8,128)(2,1)S(1)}, bf16[32,1024]{1,0:T(8,128)(2,1)}, u32[]{:S(2)}) copy-start(bf16[32,1024]{1,0:T(8,128)(2,1)} %gating_ref.1) | copy-start | bytes 196612
  17.7 10.9 %copy-start.2 = (bf16[32,1024]{1,0:T(8,128)(2,1)S(1)}, bf16[32,1024]{1,0:T(8,128)(2,1)}, u32[]{:S(2)}) copy-start(bf16[32,1024]{1,0:T(8,128)(2,1)} %cotangent_ref.1) | copy-start | bytes 196612

commit v9 on v8

--- a/solution.py
+++ b/solution.py
@@ -170,14 +170,23 @@
             ]
         )
     ]
-    for copy in copies:
+    for copy in (copies[2], *copies[:2], *copies[3:]):
         copy.start()
-    for copy in copies:
-        copy.wait()
-    signal = signal_ref[...].astype(jnp.float32)
-    gated = cotangent_ref[...].astype(jnp.float32) * gating_ref[...].astype(jnp.float32)
-    rows = tile_rows(jnp.concatenate([signal, gated, taps_ref[...]], axis=1))
-    message_ref[...] = rows.reshape(message_ref.shape).astype(jnp.bfloat16)
+    cotangent_copy, gating_copy, signal_copy, taps_copy, weight_copy = copies
+    at = length // (TILE * LANES)
+
+    def put(first, stop, values):
+        rows = tile_rows(values).reshape(channels, stop - first, TILE, LANES)
+        message_ref[:, first:stop] = rows.astype(jnp.bfloat16)
+
+    signal_copy.wait()
+    put(0, at, signal_ref[...].astype(jnp.float32))
+    cotangent_copy.wait()
+    gating_copy.wait()
+    put(at, 2 * at, cotangent_ref[...].astype(jnp.float32) * gating_ref[...].astype(jnp.float32))
+    taps_copy.wait()
+    put(2 * at, message_ref.shape[1], taps_ref[...])
+    weight_copy.wait()
     square = (channels, channels)
     diagonal = lax.broadcasted_iota(jnp.int32, square, 0) == lax.broadcasted_iota(jnp.int32, square, 1)
     weight = jnp.sum(jnp.where(diagonal, jnp.broadcast_to(weight_ref[...], square), 0.0), axis=1, keepdims=True)

time: 29.6 us -> 29.6 us (level)
  no operation moved by 1% of the time
where the time goes in v9:
time: 29.6 us; the launch traced here: 29.4 us
  blocking collectives  25.9 us (88%)
  Pallas kernels  2.68 us (9%)
  between operations  0.72 us (2%)
    all_to_all x1, blocking collectives, filter_per_device(): got = exchange(message)  15.1 us
    all_to_all x1, blocking collectives, filter_per_device(): home = exchange(result)  10.9 us
    pallas_call x1, Pallas kernels, pack(): pl.pallas_call(functools.partial(pack_kernel, groups), out_shape=(jax.Sha...  1.13 us
    pallas_call x1, Pallas kernels, spectral_products(): pl.pallas_call(functools.partial(spectral_kernel, groups, peers, scale),...  0.79 us
    pallas_call x1, Pallas kernels, finish(): pl.pallas_call(functools.partial(finish_kernel, groups), out_shape=(jax.S...  0.76 us

profile of v9, /device:TPU:0, one launch (start us, length us, event | category | flops | bytes accessed | tf_op | source)
XLA Modules:
  0.0 29.4 jit_solution(14875892869303213678)
XLA Ops:
  0.6 1.1 %pack.1 = (bf16[32,9,2,128]{3,2,1,0:T(2,128)(2,1)S(1)}, f32[32,128]{1,0:T(8,128)S(1)}) custom-call(bf16[32,1024]{1,0:T(8,128)(2,1)} %signal_ref.1, bf16[32,1024]{1,0:T(8,128)(2,1)} %gating_ref.1, bf16[32,1024]{1,0:T(8,128)(2,1)} %cotangent_ref.1, f32[32,1024]{1,0:T(8,128)} %filters_hbm.1, f32[1,32]{1,0:T(1,128)} %bitcast.1), custom_call_target="tpu_custom_call" | custom-call | tf_op jit(solution)/shard_map/pack/pallas_call | solution.py:200
  1.8 0.0 copy-start.3
  1.8 0.0 copy-start.4
  1.8 0.0 copy-start.5
  1.8 0.0 copy-start.6
  1.8 15.1 %all_to_all.10.got_ref = bf16[32,9,2,128]{3,2,1,0:T(2,128)(2,1)S(1)} all-to-all(bf16[32,9,2,128]{3,2,1,0:T(2,128)(2,1)S(1)} %get-tuple-element.5), channel_id=1, replica_groups={{0,1,24,25,16,17,8,9,4,5,28,29,20,21,12,13,2,3,26,27,18,19,10,11,6,7,30..., dimensions={0} | all-to-all | bytes 294912 | tf_op jit(solution)/shard_map/all_to_all | solution.py:264
  16.9 0.0 copy-done.3
  16.9 0.0 copy-done.4
  16.9 0.0 copy-done.5
  16.9 0.0 copy-done.6
  16.9 0.8 %spectral_products.1 = bf16[32,24,128]{2,1,0:T(8,128)(2,1)S(1)} custom-call(bf16[32,9,2,128]{3,2,1,0:T(2,128)(2,1)S(1)} %all_to_all.10.got_ref, bf16[128,128]{1,0:T(8,128)(2,1)S(1)} %copy-done.6, f32[2,64,128]{2,1,0:T(8,128)S(1)} %copy-done.4, bf16[256,256]{1,0:T(8,128)(2,1)S(1)} %copy-done.3, bf16[128,128]{1,0:T(8,128)(2,1)S(1)} %copy-done.5), custom_call_target="tpu_custom_call" | custom-call | tf_op jit(solution)/shard_map/spectral_products/pallas_call | solution.py:128
  17.7 0.0 copy-start
  17.7 0.0 copy-start.1
  17.7 0.0 copy-start.2
  17.7 10.9 %all_to_all.11.home_ref = bf16[32,24,128]{2,1,0:T(8,128)(2,1)S(1)} all-to-all(bf16[32,24,128]{2,1,0:T(8,128)(2,1)S(1)} %spectral_products.1), channel_id=1, replica_groups={{0,1,24,25,16,17,8,9,4,5,28,29,20,21,12,13,2,3,26,27,18,19,10,11,6,7,30..., dimensions={0} | all-to-all | bytes 393216 | tf_op jit(solution)/shard_map/all_to_all | solution.py:267
  28.6 0.0 copy-done
  28.6 0.0 copy-done.1
  28.6 0.0 copy-done.2
  28.6 0.8 %finish.1 = (bf16[32,1024]{1,0:T(8,128)(2,1)}, bf16[32,1024]{1,0:T(8,128)(2,1)}, f32[8,1024]{1,0:T(8,128)}) custom-call(bf16[32,24,128]{2,1,0:T(8,128)(2,1)S(1)} %all_to_all.11.home_ref, bf16[32,1024]{1,0:T(8,128)(2,1)S(1)} %copy-done, bf16[32,1024]{1,0:T(8,128)(2,1)S(1)} %copy-done.1, bf16[32,1024]{1,0:T(8,128)(2,1)S(1)} %copy-done.2, ...), custom_call_target="tpu_custom_call" | custom-call | tf_op jit(solution)/shard_map/finish/pallas_call | solution.py:238
Async XLA Ops:
  1.8 15.1 %copy-start.3 = (bf16[256,256]{1,0:T(8,128)(2,1)S(1)}, bf16[256,256]{1,0:T(8,128)(2,1)}, u32[]{:S(2)}) copy-start(bf16[256,256]{1,0:T(8,128)(2,1)} %constant.10.clone.second_ref) | copy-start | bytes 393220
  1.8 15.1 %copy-start.4 = (f32[2,64,128]{2,1,0:T(8,128)S(1)}, f32[2,64,128]{2,1,0:T(8,128)}, u32[]{:S(2)}) copy-start(f32[2,64,128]{2,1,0:T(8,128)} %constant.9.clone.twiddle_ref) | copy-start | bytes 196612
  1.8 15.1 %copy-start.5 = (bf16[128,128]{1,0:T(8,128)(2,1)S(1)}, bf16[128,128]{1,0:T(8,128)(2,1)}, u32[]{:S(2)}) copy-start(bf16[128,128]{1,0:T(8,128)(2,1)} %constant.11.clone.last_ref) | copy-start | bytes 98308
  1.8 15.1 %copy-start.6 = (bf16[128,128]{1,0:T(8,128)(2,1)S(1)}, bf16[128,128]{1,0:T(8,128)(2,1)}, u32[]{:S(2)}) copy-start(bf16[128,128]{1,0:T(8,128)(2,1)} %constant.8.clone.first_ref) | copy-start | bytes 98308
  17.7 10.9 %copy-start = (bf16[32,1024]{1,0:T(8,128)(2,1)S(1)}, bf16[32,1024]{1,0:T(8,128)(2,1)}, u32[]{:S(2)}) copy-start(bf16[32,1024]{1,0:T(8,128)(2,1)} %signal_ref.1) | copy-start | bytes 196612
  17.7 10.9 %copy-start.1 = (bf16[32,1024]{1,0:T(8,128)(2,1)S(1)}, bf16[32,1024]{1,0:T(8,128)(2,1)}, u32[]{:S(2)}) copy-start(bf16[32,1024]{1,0:T(8,128)(2,1)} %gating_ref.1) | copy-start | bytes 196612
  17.7 10.9 %copy-start.2 = (bf16[32,1024]{1,0:T(8,128)(2,1)S(1)}, bf16[32,1024]{1,0:T(8,128)(2,1)}, u32[]{:S(2)}) copy-start(bf16[32,1024]{1,0:T(8,128)(2,1)} %cotangent_ref.1) | copy-start | bytes 196612

commit v10 on v9

--- a/solution.py
+++ b/solution.py
@@ -27,14 +27,14 @@
     n2 = np.arange(LANES)
     outer = np.pi * (np.outer(2 * k1 + 1, n1) % (2 * height)) / height
     high, low = split_table(np.concatenate([np.cos(outer), -np.sin(outer)], axis=0))
-    first = np.concatenate([high, low], axis=1)
+    first = high
     turn = np.pi * (np.outer(2 * k1 + 1, n2) % (2 * padded)) / padded
     twiddle = np.stack([np.cos(turn), np.sin(turn)]).astype(np.float32)
     inner = 2.0 * np.pi * (np.outer(n2, n2) % LANES) / LANES
     cosine, sine = np.cos(inner), np.sin(inner)
     second = np.block([[cosine, -sine], [sine, cosine]]).astype(jnp.bfloat16)
     high, low = split_table(np.concatenate([np.cos(outer.T), -np.sin(outer.T)], axis=1) * (2.0 / padded))
-    last = np.concatenate([high, low], axis=0)
+    last = high
     return first, twiddle, second, last
 
 
@@ -75,7 +75,7 @@
     second = second_ref[...]
 
     def first_stage(values):
-        return dot(first_ref[...], jnp.concatenate([values, values], axis=0))
+        return dot(first_ref[...], values)
 
     def turn_forward(stage):
         parts = []
@@ -98,8 +98,7 @@
         for imag, real in swapped_pairs:
             turned = jnp.concatenate([real * cosine - imag * sine, imag * cosine + real * sine], axis=0)
             parts.append(turned.astype(jnp.bfloat16))
-        both = dot(last_ref[...], jnp.concatenate(parts, axis=1))
-        return both[:rows] + both[rows:]
+        return dot(last_ref[...], jnp.concatenate(parts, axis=1))
 
     taps_in = jnp.concatenate([part[2 * piece : 2 * piece + taps] for part in got], axis=0).astype(jnp.bfloat16)
     signal_in = jnp.concatenate([gather(group, 0) for group in range(groups)] + [taps_in], axis=1)

time: 29.6 us -> 29.6 us (level)
  no operation moved by 1% of the time
where the time goes in v10:
time: 29.6 us; the launch traced here: 29.4 us
  blocking collectives  25.9 us (88%)
  Pallas kernels  2.66 us (9%)
  between operations  0.72 us (2%)
    all_to_all x1, blocking collectives, filter_per_device(): got = exchange(message)  15.1 us
    all_to_all x1, blocking collectives, filter_per_device(): home = exchange(result)  10.9 us
    pallas_call x1, Pallas kernels, pack(): pl.pallas_call(functools.partial(pack_kernel, groups), out_shape=(jax.Sha...  1.13 us
    pallas_call x1, Pallas kernels, spectral_products(): pl.pallas_call(functools.partial(spectral_kernel, groups, peers, scale),...  0.77 us
    pallas_call x1, Pallas kernels, finish(): pl.pallas_call(functools.partial(finish_kernel, groups), out_shape=(jax.S...  0.76 us

profile of v10, /device:TPU:0, one launch (start us, length us, event | category | flops | bytes accessed | tf_op | source)
XLA Modules:
  0.0 29.4 jit_solution(6807785419631826941)
XLA Ops:
  0.6 1.1 %pack.1 = (bf16[32,9,2,128]{3,2,1,0:T(2,128)(2,1)S(1)}, f32[32,128]{1,0:T(8,128)S(1)}) custom-call(bf16[32,1024]{1,0:T(8,128)(2,1)} %signal_ref.1, bf16[32,1024]{1,0:T(8,128)(2,1)} %gating_ref.1, bf16[32,1024]{1,0:T(8,128)(2,1)} %cotangent_ref.1, f32[32,1024]{1,0:T(8,128)} %filters_hbm.1, f32[1,32]{1,0:T(1,128)} %bitcast.1), custom_call_target="tpu_custom_call" | custom-call | tf_op jit(solution)/shard_map/pack/pallas_call | solution.py:199
  1.8 0.0 copy-start.3
  1.8 0.0 copy-start.4
  1.8 0.0 copy-start.5
  1.8 0.0 copy-start.6
  1.8 15.1 %all_to_all.10.got_ref = bf16[32,9,2,128]{3,2,1,0:T(2,128)(2,1)S(1)} all-to-all(bf16[32,9,2,128]{3,2,1,0:T(2,128)(2,1)S(1)} %get-tuple-element.5), channel_id=1, replica_groups={{0,1,24,25,16,17,8,9,4,5,28,29,20,21,12,13,2,3,26,27,18,19,10,11,6,7,30..., dimensions={0} | all-to-all | bytes 294912 | tf_op jit(solution)/shard_map/all_to_all | solution.py:263
  16.9 0.0 copy-done.3
  16.9 0.0 copy-done.4
  16.9 0.0 copy-done.5
  16.9 0.0 copy-done.6
  16.9 0.8 %spectral_products.1 = bf16[32,24,128]{2,1,0:T(8,128)(2,1)S(1)} custom-call(bf16[32,9,2,128]{3,2,1,0:T(2,128)(2,1)S(1)} %all_to_all.10.got_ref, bf16[128,64]{1,0:T(8,128)(2,1)S(1)} %copy-done.5, f32[2,64,128]{2,1,0:T(8,128)S(1)} %copy-done.4, bf16[256,256]{1,0:T(8,128)(2,1)S(1)} %copy-done.3, bf16[64,128]{1,0:T(8,128)(2,1)S(1)} %copy-done.6), custom_call_target="tpu_custom_call" | custom-call | tf_op jit(solution)/shard_map/spectral_products/pallas_call | solution.py:127
  17.7 0.0 copy-start
  17.7 0.0 copy-start.1
  17.7 0.0 copy-start.2
  17.7 10.9 %all_to_all.11.home_ref = bf16[32,24,128]{2,1,0:T(8,128)(2,1)S(1)} all-to-all(bf16[32,24,128]{2,1,0:T(8,128)(2,1)S(1)} %spectral_products.1), channel_id=1, replica_groups={{0,1,24,25,16,17,8,9,4,5,28,29,20,21,12,13,2,3,26,27,18,19,10,11,6,7,30..., dimensions={0} | all-to-all | bytes 393216 | tf_op jit(solution)/shard_map/all_to_all | solution.py:266
  28.6 0.0 copy-done
  28.6 0.0 copy-done.1
  28.6 0.0 copy-done.2
  28.6 0.8 %finish.1 = (bf16[32,1024]{1,0:T(8,128)(2,1)}, bf16[32,1024]{1,0:T(8,128)(2,1)}, f32[8,1024]{1,0:T(8,128)}) custom-call(bf16[32,24,128]{2,1,0:T(8,128)(2,1)S(1)} %all_to_all.11.home_ref, bf16[32,1024]{1,0:T(8,128)(2,1)S(1)} %copy-done, bf16[32,1024]{1,0:T(8,128)(2,1)S(1)} %copy-done.1, bf16[32,1024]{1,0:T(8,128)(2,1)S(1)} %copy-done.2, ...), custom_call_target="tpu_custom_call" | custom-call | tf_op jit(solution)/shard_map/finish/pallas_call | solution.py:237
Async XLA Ops:
  1.8 15.1 %copy-start.3 = (bf16[256,256]{1,0:T(8,128)(2,1)S(1)}, bf16[256,256]{1,0:T(8,128)(2,1)}, u32[]{:S(2)}) copy-start(bf16[256,256]{1,0:T(8,128)(2,1)} %constant.10.clone.second_ref) | copy-start | bytes 393220
  1.8 15.1 %copy-start.4 = (f32[2,64,128]{2,1,0:T(8,128)S(1)}, f32[2,64,128]{2,1,0:T(8,128)}, u32[]{:S(2)}) copy-start(f32[2,64,128]{2,1,0:T(8,128)} %constant.9.clone.twiddle_ref) | copy-start | bytes 196612
  1.8 15.1 %copy-start.5 = (bf16[128,64]{1,0:T(8,128)(2,1)S(1)}, bf16[128,64]{1,0:T(8,128)(2,1)}, u32[]{:S(2)}) copy-start(bf16[128,64]{1,0:T(8,128)(2,1)} %constant.8.clone.first_ref) | copy-start | bytes 49156
  1.8 15.1 %copy-start.6 = (bf16[64,128]{1,0:T(8,128)(2,1)S(1)}, bf16[64,128]{1,0:T(8,128)(2,1)}, u32[]{:S(2)}) copy-start(bf16[64,128]{1,0:T(8,128)(2,1)} %constant.11.clone.last_ref) | copy-start | bytes 49156
  17.7 10.9 %copy-start = (bf16[32,1024]{1,0:T(8,128)(2,1)S(1)}, bf16[32,1024]{1,0:T(8,128)(2,1)}, u32[]{:S(2)}) copy-start(bf16[32,1024]{1,0:T(8,128)(2,1)} %signal_ref.1) | copy-start | bytes 196612
  17.7 10.9 %copy-start.1 = (bf16[32,1024]{1,0:T(8,128)(2,1)S(1)}, bf16[32,1024]{1,0:T(8,128)(2,1)}, u32[]{:S(2)}) copy-start(bf16[32,1024]{1,0:T(8,128)(2,1)} %gating_ref.1) | copy-start | bytes 196612
  17.7 10.9 %copy-start.2 = (bf16[32,1024]{1,0:T(8,128)(2,1)S(1)}, bf16[32,1024]{1,0:T(8,128)(2,1)}, u32[]{:S(2)}) copy-start(bf16[32,1024]{1,0:T(8,128)(2,1)} %cotangent_ref.1) | copy-start | bytes 196612

commit v11 on v9

--- a/solution.py
+++ b/solution.py
@@ -45,11 +45,12 @@
 def slot_order(peers, groups):
     if peers % 2 or groups % 2:
         return list(range(peers * groups))
+    outer = list(reversed(range(peers // 2)))
     return [
         (high * 2 + low) * groups + (plane * 2 + core)
         for plane in range(groups // 2)
         for low in range(2)
-        for high in [0, *reversed(range(1, peers // 2))]
+        for high in [*outer[-2:], *outer[:-2]]
         for core in range(2)
     ]
 

time: 29.6 us -> 29.6 us (level)
  no operation moved by 1% of the time
where the time goes in v11:
time: 29.6 us; the launch traced here: 29.4 us
  blocking collectives  25.9 us (88%)
  Pallas kernels  2.68 us (9%)
  between operations  0.72 us (2%)
    all_to_all x1, blocking collectives, filter_per_device(): got = exchange(message)  15.1 us
    all_to_all x1, blocking collectives, filter_per_device(): home = exchange(result)  10.9 us
    pallas_call x1, Pallas kernels, pack(): pl.pallas_call(functools.partial(pack_kernel, groups), out_shape=(jax.Sha...  1.13 us
    pallas_call x1, Pallas kernels, spectral_products(): pl.pallas_call(functools.partial(spectral_kernel, groups, peers, scale),...  0.79 us
    pallas_call x1, Pallas kernels, finish(): pl.pallas_call(functools.partial(finish_kernel, groups), out_shape=(jax.S...  0.76 us

profile of v11, /device:TPU:0, one launch (start us, length us, event | category | flops | bytes accessed | tf_op | source)
XLA Modules:
  0.0 29.4 jit_solution(8107529852927002972)
XLA Ops:
  0.6 1.1 %pack.1 = (bf16[32,9,2,128]{3,2,1,0:T(2,128)(2,1)S(1)}, f32[32,128]{1,0:T(8,128)S(1)}) custom-call(bf16[32,1024]{1,0:T(8,128)(2,1)} %signal_ref.1, bf16[32,1024]{1,0:T(8,128)(2,1)} %gating_ref.1, bf16[32,1024]{1,0:T(8,128)(2,1)} %cotangent_ref.1, f32[32,1024]{1,0:T(8,128)} %filters_hbm.1, f32[1,32]{1,0:T(1,128)} %bitcast.1), custom_call_target="tpu_custom_call" | custom-call | tf_op jit(solution)/shard_map/pack/pallas_call | solution.py:201
  1.8 0.0 copy-start.3
  1.8 0.0 copy-start.4
  1.8 0.0 copy-start.5
  1.8 0.0 copy-start.6
  1.8 15.1 %all_to_all.10.got_ref = bf16[32,9,2,128]{3,2,1,0:T(2,128)(2,1)S(1)} all-to-all(bf16[32,9,2,128]{3,2,1,0:T(2,128)(2,1)S(1)} %get-tuple-element.5), channel_id=1, replica_groups={{8,9,0,1,24,25,16,17,12,13,4,5,28,29,20,21,10,11,2,3,26,27,18,19,14,15,..., dimensions={0} | all-to-all | bytes 294912 | tf_op jit(solution)/shard_map/all_to_all | solution.py:265
  16.9 0.0 copy-done.3
  16.9 0.0 copy-done.4
  16.9 0.0 copy-done.5
  16.9 0.0 copy-done.6
  16.9 0.8 %spectral_products.1 = bf16[32,24,128]{2,1,0:T(8,128)(2,1)S(1)} custom-call(bf16[32,9,2,128]{3,2,1,0:T(2,128)(2,1)S(1)} %all_to_all.10.got_ref, bf16[128,128]{1,0:T(8,128)(2,1)S(1)} %copy-done.6, f32[2,64,128]{2,1,0:T(8,128)S(1)} %copy-done.4, bf16[256,256]{1,0:T(8,128)(2,1)S(1)} %copy-done.3, bf16[128,128]{1,0:T(8,128)(2,1)S(1)} %copy-done.5), custom_call_target="tpu_custom_call" | custom-call | tf_op jit(solution)/shard_map/spectral_products/pallas_call | solution.py:129
  17.7 0.0 copy-start
  17.7 0.0 copy-start.1
  17.7 0.0 copy-start.2
  17.7 10.9 %all_to_all.11.home_ref = bf16[32,24,128]{2,1,0:T(8,128)(2,1)S(1)} all-to-all(bf16[32,24,128]{2,1,0:T(8,128)(2,1)S(1)} %spectral_products.1), channel_id=1, replica_groups={{8,9,0,1,24,25,16,17,12,13,4,5,28,29,20,21,10,11,2,3,26,27,18,19,14,15,..., dimensions={0} | all-to-all | bytes 393216 | tf_op jit(solution)/shard_map/all_to_all | solution.py:268
  28.6 0.0 copy-done
  28.6 0.0 copy-done.1
  28.6 0.0 copy-done.2
  28.6 0.8 %finish.1 = (bf16[32,1024]{1,0:T(8,128)(2,1)}, bf16[32,1024]{1,0:T(8,128)(2,1)}, f32[8,1024]{1,0:T(8,128)}) custom-call(bf16[32,24,128]{2,1,0:T(8,128)(2,1)S(1)} %all_to_all.11.home_ref, bf16[32,1024]{1,0:T(8,128)(2,1)S(1)} %copy-done, bf16[32,1024]{1,0:T(8,128)(2,1)S(1)} %copy-done.1, bf16[32,1024]{1,0:T(8,128)(2,1)S(1)} %copy-done.2, ...), custom_call_target="tpu_custom_call" | custom-call | tf_op jit(solution)/shard_map/finish/pallas_call | solution.py:239
Async XLA Ops:
  1.8 15.1 %copy-start.3 = (bf16[256,256]{1,0:T(8,128)(2,1)S(1)}, bf16[256,256]{1,0:T(8,128)(2,1)}, u32[]{:S(2)}) copy-start(bf16[256,256]{1,0:T(8,128)(2,1)} %constant.10.clone.second_ref) | copy-start | bytes 393220
  1.8 15.1 %copy-start.4 = (f32[2,64,128]{2,1,0:T(8,128)S(1)}, f32[2,64,128]{2,1,0:T(8,128)}, u32[]{:S(2)}) copy-start(f32[2,64,128]{2,1,0:T(8,128)} %constant.9.clone.twiddle_ref) | copy-start | bytes 196612
  1.8 15.1 %copy-start.5 = (bf16[128,128]{1,0:T(8,128)(2,1)S(1)}, bf16[128,128]{1,0:T(8,128)(2,1)}, u32[]{:S(2)}) copy-start(bf16[128,128]{1,0:T(8,128)(2,1)} %constant.11.clone.last_ref) | copy-start | bytes 98308
  1.8 15.1 %copy-start.6 = (bf16[128,128]{1,0:T(8,128)(2,1)S(1)}, bf16[128,128]{1,0:T(8,128)(2,1)}, u32[]{:S(2)}) copy-start(bf16[128,128]{1,0:T(8,128)(2,1)} %constant.8.clone.first_ref) | copy-start | bytes 98308
  17.7 10.9 %copy-start = (bf16[32,1024]{1,0:T(8,128)(2,1)S(1)}, bf16[32,1024]{1,0:T(8,128)(2,1)}, u32[]{:S(2)}) copy-start(bf16[32,1024]{1,0:T(8,128)(2,1)} %signal_ref.1) | copy-start | bytes 196612
  17.7 10.9 %copy-start.1 = (bf16[32,1024]{1,0:T(8,128)(2,1)S(1)}, bf16[32,1024]{1,0:T(8,128)(2,1)}, u32[]{:S(2)}) copy-start(bf16[32,1024]{1,0:T(8,128)(2,1)} %gating_ref.1) | copy-start | bytes 196612
  17.7 10.9 %copy-start.2 = (bf16[32,1024]{1,0:T(8,128)(2,1)S(1)}, bf16[32,1024]{1,0:T(8,128)(2,1)}, u32[]{:S(2)}) copy-start(bf16[32,1024]{1,0:T(8,128)(2,1)} %cotangent_ref.1) | copy-start | bytes 196612
